TPU v7x, 1024 devices: a whole 4x8x16 slice. The times are simulated.
1024 devices in a mesh: gx: 16 (over y, core), gy: 16 (over z_hi, x), gz: 4 (over z_lo).
Axes of the slice: x: 4, y: 8, z: 16 (z_hi: 4, z_lo: 4; z = z_hi * 4 + z_lo), core: 2. Of those that a mesh axis runs over, the one named last changes fastest.
Arguments:
- positions: float32 [3, 16, 16, 4, 192], P(None, 'gx', 'gy', 'gz'), may hold values from 0 to 8, as said below
- polarizability: float32 [16, 16, 4, 192], P('gx', 'gy', 'gz'), may hold values from 0.01 to 0.06
- direct_field: float32 [3, 16, 16, 4, 192], P(None, 'gx', 'gy', 'gz'), may hold values from -150 to 150
- groups: int32 [16, 16, 4, 192], P('gx', 'gy', 'gz'), may hold values from 0 to 47, never falling along the last dimension, each value on 1 to 8 neighbouring positions
Outputs:
- dipoles: float32 [3, 16, 16, 4, 192], P(None, 'gx', 'gy', 'gz')
- gradient: float32 [3, 16, 16, 4, 192], P(None, 'gx', 'gy', 'gz')
- energy: float32 [], replicated
Inputs may be any that keep to these rules, and one draw needn't show every extreme that they name: `positions`: atoms of a domain sit one to a lattice site of 8 x 8 x 3 sites of spacing 1, in the order x, y, normal (the normal fastest), each within 0.2 of its site along every component, so no two atoms are closer than 0.6. `groups`: along the atoms of one domain the ids never fall; each group holds 1 to 8 atoms.
All inputs are finite; a program needn't handle non-finite values.
Results may differ from a plain program's by a relative error of at most 0.0003.
Values sent between devices are 32-bit elements; how exact they have to be, the bound alone decides.
No kernel may reach another device: no remote copies, remote signals or barrier semaphores. Data moves between devices by JAX's collectives and lax.ppermute only.
A program may use at most 32 MiB of HBM per device.

v0:
```python
import functools

import jax
import jax.numpy as jnp
from jax import lax
from jax.sharding import Mesh
from jax.sharding import PartitionSpec as P

LX = 8
LY = 8
DEPTH = 3
CUTOFF = 3
GX_GY_GZ = ("gx_0", "gx_1", "gy_0", "gy_1", "gz")
GX = ("gx_0", "gx_1")
GY = ("gy_0", "gy_1")


thole_factor = 0.39
group_scale = 0.5


def padded(cells, sides, width):
    for axis, dim in sides:
        count = lax.axis_size(axis)
        head = lax.slice_in_dim(cells, 0, width, axis=dim)
        tail = lax.slice_in_dim(cells, cells.shape[dim] - width, cells.shape[dim], axis=dim)
        cells = jnp.concatenate(
            [
                lax.ppermute(tail, axis, [(i, (i + 1) % count) for i in range(count)]),
                cells,
                lax.ppermute(head, axis, [((i + 1) % count, i) for i in range(count)]),
            ],
            axis=dim,
        )
    return cells


def one_axis_at_a_time(value, axes):
    return functools.reduce(lax.psum, axes, value)


def tensor_parts(own_pos, own_polar, own_group, own_site, far_pos, far_polar, far_group, far_ident):
    displace = far_pos[:, None, :] - own_pos[:, :, None]
    dist_sq = jnp.sum(displace * displace, axis=0)
    same_atom = own_site[:, None] == far_ident[None, :]
    same_group = jnp.logical_and(far_ident[None, :] >= 0, own_group[:, None] == far_group[None, :])
    safe_sq = jnp.where(same_atom, 1.0, dist_sq)
    inverse = lax.rsqrt(safe_sq)
    cut_ratio = safe_sq / (CUTOFF * CUTOFF)
    smooth_cut = jnp.where(cut_ratio < 1.0, jnp.square(1.0 - cut_ratio), 0.0)
    damping = (
        thole_factor
        * safe_sq
        * safe_sq
        * inverse
        / jnp.sqrt(own_polar[:, None] * far_polar[None, :])
    )
    decayed = jnp.exp(-damping)
    damp_three = -jnp.expm1(-damping)
    damp_five = damp_three - damping * decayed
    weight = smooth_cut * jnp.where(same_group, group_scale, 1.0) * jnp.where(same_atom, 0.0, 1.0)
    inv_cube = inverse * inverse * inverse
    coupling3 = weight * damp_three * inv_cube
    coupling5 = 3.0 * weight * damp_five * inv_cube * inverse * inverse
    return (displace, coupling3, coupling5)


def apply_tensor(
    own_pos, own_polar, own_group, own_site, far_pos, far_polar, far_group, far_ident, far_vector
):
    atom_count = own_pos.shape[1]

    def apply_advance(running, slot_item):
        pos_slot, polar_slot, group_slot, ident_slot, vector_slot = slot_item
        displace, coupling3, coupling5 = tensor_parts(
            own_pos, own_polar, own_group, own_site, pos_slot, polar_slot, group_slot, ident_slot
        )
        along = jnp.sum(displace * vector_slot[:, None, :], axis=0)
        contrib = jnp.sum(
            coupling5[None] * displace * along[None] - coupling3[None] * vector_slot[:, None, :],
            axis=2,
        )
        return (running + contrib, None)

    result, _ = lax.scan(
        apply_advance,
        jnp.zeros((3, atom_count), jnp.float32),
        (far_pos, far_polar, far_group, far_ident, far_vector),
    )
    return result


def pair_gradient(
    own_pos,
    own_polar,
    own_group,
    own_site,
    far_pos,
    far_polar,
    far_group,
    far_ident,
    own_dip,
    own_adj,
    far_dip,
    far_adj,
):

    def slot_value(position, pos_slot, polar_slot, group_slot, ident_slot, dip_slot, adj_slot):
        displace, coupling3, coupling5 = tensor_parts(
            position, own_polar, own_group, own_site, pos_slot, polar_slot, group_slot, ident_slot
        )
        own_dip_along = jnp.sum(displace * own_dip[:, :, None], axis=0)
        own_adj_along = jnp.sum(displace * own_adj[:, :, None], axis=0)
        far_dip_along = jnp.sum(displace * dip_slot[:, None, :], axis=0)
        far_adj_along = jnp.sum(displace * adj_slot[:, None, :], axis=0)
        cross_terms = jnp.sum(
            own_dip[:, :, None] * adj_slot[:, None, :] + own_adj[:, :, None] * dip_slot[:, None, :],
            axis=0,
        )
        return 0.5 * jnp.sum(
            coupling5 * (own_dip_along * far_adj_along + own_adj_along * far_dip_along)
            - coupling3 * cross_terms
        )

    def pair_advance(running, slot_item):
        pos_slot, polar_slot, group_slot, ident_slot, dip_slot, adj_slot = slot_item
        return (
            running
            + jax.grad(slot_value)(
                own_pos, pos_slot, polar_slot, group_slot, ident_slot, dip_slot, adj_slot
            ),
            None,
        )

    result, _ = lax.scan(
        pair_advance,
        jnp.zeros(own_pos.shape, jnp.float32),
        (far_pos, far_polar, far_group, far_ident, far_dip, far_adj),
    )
    return result


def edge_shift(extent, inner):
    place = jnp.arange(extent + 2 * CUTOFF, dtype=jnp.int32)
    return jnp.where(place < CUTOFF, -inner, jnp.where(place >= CUTOFF + inner, inner, 0))


def on_device(positions, polarizability, direct_field, groups):
    atom_count = positions.shape[-1]
    own_pos = positions.reshape(3, atom_count)
    polar = polarizability.reshape(atom_count)
    direct = direct_field.reshape(3, atom_count)
    own_group = groups.reshape(atom_count)
    own_site = jnp.arange(atom_count, dtype=jnp.int32)
    frame = jnp.concatenate([positions, polarizability[None]], axis=0).reshape(4, LX, LY, DEPTH)
    framed = padded(frame, ((GX, 1), (GY, 2), ("gz", 3)), CUTOFF)
    wide_x = LX + 2 * CUTOFF
    shape_ext = (wide_x, LY + 2 * CUTOFF, DEPTH + 2 * CUTOFF)
    offsets = jnp.stack(
        [
            jnp.broadcast_to(edge_shift(LX, LX)[:, None, None], shape_ext),
            jnp.broadcast_to(edge_shift(LY, LY)[None, :, None], shape_ext),
            jnp.broadcast_to(edge_shift(DEPTH, DEPTH)[None, None, :], shape_ext),
        ]
    ).astype(jnp.float32)
    far_pos = (framed[:3] + offsets).reshape(3, wide_x, -1).transpose(1, 0, 2)
    far_polar = framed[3].reshape(wide_x, -1)
    far_ident = jnp.pad(own_site.reshape(LX, LY, DEPTH), CUTOFF, constant_values=-1).reshape(
        wide_x, -1
    )
    far_group = jnp.pad(own_group.reshape(LX, LY, DEPTH), CUTOFF, constant_values=-1).reshape(
        wide_x, -1
    )

    def neighbours(vector):
        channels = vector.shape[0]
        lattice = vector.reshape(channels, LX, LY, DEPTH)
        cycle = padded(lattice, ((GX, 1), (GY, 2), ("gz", 3)), CUTOFF)
        return cycle.reshape(channels, cycle.shape[1], -1).transpose(1, 0, 2)

    def apply_local(ghosts):
        return apply_tensor(
            own_pos, polar, own_group, own_site, far_pos, far_polar, far_group, far_ident, ghosts
        )

    dipole_start = polar * direct
    ghosts_start = neighbours(dipole_start)
    image_start = apply_local(ghosts_start)
    precond_start = polar * image_start
    ghosts_first = neighbours(precond_start)
    tensor_first = apply_local(ghosts_first)
    image_first = precond_start / polar - tensor_first
    norm_first, curve_first, cross_first, square_first = (
        one_axis_at_a_time(jnp.sum(image_start * precond_start), GX_GY_GZ),
        one_axis_at_a_time(jnp.sum(precond_start * image_first), GX_GY_GZ),
        one_axis_at_a_time(jnp.sum(image_start * polar * image_first), GX_GY_GZ),
        one_axis_at_a_time(jnp.sum(image_first * polar * image_first), GX_GY_GZ),
    )
    gamma_first = norm_first / curve_first
    resid_mid = image_start - gamma_first * image_first
    precond_mid = polar * resid_mid
    norm_mid = (
        norm_first - 2.0 * gamma_first * cross_first + gamma_first * gamma_first * square_first
    )
    dipole_mid = dipole_start + gamma_first * precond_start
    search_second = precond_mid + norm_mid / norm_first * precond_start
    ghosts_second = neighbours(search_second)
    tensor_second = apply_local(ghosts_second)
    image_second = search_second / polar - tensor_second
    curve_second, mid_energy, search_energy = (
        one_axis_at_a_time(jnp.sum(search_second * image_second), GX_GY_GZ),
        one_axis_at_a_time(jnp.sum(dipole_mid * direct), GX_GY_GZ),
        one_axis_at_a_time(jnp.sum(search_second * direct), GX_GY_GZ),
    )
    gamma_second = norm_mid / curve_second
    dipoles = dipole_mid + gamma_second * search_second
    devices_all = lax.axis_size(GX) * lax.axis_size(GY) * lax.axis_size("gz")
    energy = -(mid_energy + gamma_second * search_energy) / (2.0 * atom_count * devices_all)
    tensor_final = image_start + gamma_first * tensor_first + gamma_second * tensor_second
    adjoint = polar * direct + polar * tensor_final
    far_dip = ghosts_start + gamma_first * ghosts_first + gamma_second * ghosts_second
    far_adj = neighbours(adjoint)
    gradient = pair_gradient(
        own_pos,
        polar,
        own_group,
        own_site,
        far_pos,
        far_polar,
        far_group,
        far_ident,
        dipoles,
        adjoint,
        far_dip,
        far_adj,
    )
    return (
        dipoles.reshape(3, 1, 1, 1, atom_count),
        gradient.reshape(3, 1, 1, 1, atom_count),
        energy,
    )


def solution(mesh):
    split = Mesh(
        mesh.devices.reshape(8, 2, 4, 4, mesh.shape["gz"]), ("gx_0", "gx_1", "gy_0", "gy_1", "gz")
    )
    return jax.shard_map(
        on_device,
        mesh=split,
        in_specs=(
            P(None, GX, GY, "gz", None),
            P(GX, GY, "gz", None),
            P(None, GX, GY, "gz", None),
            P(GX, GY, "gz", None),
        ),
        out_specs=(P(None, GX, GY, "gz", None), P(None, GX, GY, "gz", None), P()),
        check_vma=False,
    )
```

profile of v0, /device:TPU:6, one launch (start us, length us, event | category | flops | bytes accessed | tf_op | source)
XLA Modules:
  0.0 354.4 jit_solution(12855999576466058204)
XLA Ops:
  12.1 10.8 %collective-permute-start.8 = (f32[3,14,3,3]{3,2,1,0:T(4,128)S(1)}, f32[3,14,3,3]{3,2,1,0:T(4,128)S(1)}, u32[]{:S(2)}, u32[]{:S(2)}) collective-permute-start(f32[3,14,3,3]{3,2,1,0:T(4,128)S(1)} %get-tuple-element.698), channel_id=1, source_target_pairs={{0,4},{4,8},{8,12},{12,16},{16,20},{20,24},{24,28},{28,32},{32,36}... | collective-permute-start | bytes 4544 | tf_op jit(solution)/shard_map/ppermute | solution.py:29
  25.3 9.9 %collective-permute-start.2 = (f32[4,14,3,3]{3,2,1,0:T(4,128)S(1)}, f32[4,14,3,3]{3,2,1,0:T(4,128)S(1)}, u32[]{:S(2)}, u32[]{:S(2)}) collective-permute-start(f32[4,14,3,3]{3,2,1,0:T(4,128)S(1)} %get-tuple-element.690), channel_id=1, source_target_pairs={{0,4},{4,8},{8,12},{12,16},{16,20},{20,24},{24,28},{28,32},{32,36}... | collective-permute-start | bytes 6056 | tf_op jit(solution)/shard_map/ppermute | solution.py:29
  39.6 6.5 %collective-permute-start.11 = (f32[3,14,14,3]{2,1,3,0:T(8,128)S(1)}, f32[3,14,14,3]{2,1,3,0:T(8,128)S(1)}, u32[]{:S(2)}, u32[]{:S(2)}) collective-permute-start(f32[3,14,14,3]{2,1,3,0:T(8,128)S(1)} %pad_maximum_fusion.8), channel_id=1, source_target_pairs={{1,0},{2,1},{3,2},{0,3},{5,4},{6,5},{7,6},{4,7},{9,8},{10,9},{11,1... | collective-permute-start | bytes 21176 | tf_op jit(solution)/shard_map/ppermute | solution.py:31
  52.4 10.4 %collective-permute-start.5 = (f32[4,14,14,3]{2,0,3,1:T(4,128)S(1)}, f32[4,14,14,3]{2,0,3,1:T(4,128)S(1)}, u32[]{:S(2)}, u32[]{:S(2)}) collective-permute-start(f32[4,14,14,3]{2,0,3,1:T(4,128)S(1)} %pad_maximum_fusion.7), channel_id=1, source_target_pairs={{1,0},{2,1},{3,2},{0,3},{5,4},{6,5},{7,6},{4,7},{9,8},{10,9},{11,1... | collective-permute-start | bytes 28232 | tf_op jit(solution)/shard_map/ppermute | solution.py:31
  65.5 5.6 %collective-permute-done.4 = f32[4,14,14,3]{2,0,3,1:T(4,128)S(1)} collective-permute-done((f32[4,14,14,3]{2,0,3,1:T(4,128)S(1)}, f32[4,14,14,3]{2,0,3,1:T(4,128)S(1)}, u32[]{:S(2)}, u32[]{:S(2)}) %collective-permute-start.4) | collective-permute-done | bytes 9440 | tf_op jit(solution)/shard_map/ppermute | solution.py:29
  72.7 11.1 %while.44 = (s32[]{:T(128)}, f32[3,192]{1,0:T(4,128)S(1)}, s32[14,126]{1,0:T(8,128)S(1)}, f32[14,3,126]{2,1,0:T(4,128)S(1)}, f32[3,1,1,1,192]{4,0,3,2,1:T(4,128)...) while((s32[]{:T(128)}, f32[3,192]{1,0:T(4,128)S(1)}, ...), condition=%wide.region_4.5_spmd.clone, body=%wide.region_0.4_spmd.clone.sunk | while | flops 1500609 | bytes 810071 | solution.py:85
  96.4 7.1 %collective-permute-done.15 = f32[3,14,3,3]{3,2,1,0:T(4,128)S(1)} collective-permute-done((f32[3,14,3,3]{3,2,1,0:T(4,128)S(1)}, f32[3,14,3,3]{3,2,1,0:T(4,128)S(1)}, u32[]{:S(2)}, u32[]{:S(2)}) %collective-permute-start.15) | collective-permute-done | bytes 1544 | tf_op jit(solution)/shard_map/ppermute | solution.py:31
  114.7 11.1 %while.45 = (s32[]{:T(128)}, f32[3,192]{1,0:T(4,128)S(1)}, s32[14,126]{1,0:T(8,128)S(1)}, f32[14,3,126]{2,1,0:T(4,128)S(1)}, f32[3,1,1,1,192]{4,0,3,2,1:T(4,128)...) while((s32[]{:T(128)}, f32[3,192]{1,0:T(4,128)S(1)}, ...), condition=%wide.region_15.16_spmd.clone, body=%wide.region_11.15_spmd.clone.sunk | while | flops 1500609 | bytes 810071 | solution.py:85
  126.4 18.7 %all-reduce.3 = (f32[]{:T(128)}, f32[]{:T(128)}, f32[]{:T(128)}) all-reduce(f32[]{:T(128)} %get-tuple-element.542, f32[]{:T(128)} %get-tuple-element.541, f32[]{:T(128)} %get-tuple-element.540), channel_id=1, replica_groups=mesh['gx_0'=8,'gx_1'=2,'gy_0'=4,'gy_1'=4,'gz'=4] {'gx_0'}, use_global_device_ids=true, to_apply=%region_6.7 | all-reduce | flops 3 | bytes 24 | tf_op jit(solution)/shard_map/psum | solution.py:39
  148.1 17.3 %all-reduce.9 = (f32[]{:T(128)}, f32[]{:T(128)}, f32[]{:T(128)}) all-reduce(f32[]{:T(128)} %get-tuple-element.659, f32[]{:T(128)} %get-tuple-element.660, f32[]{:T(128)} %get-tuple-element.661), channel_id=1, replica_groups=mesh['gx_0'=8,'gx_1'=2,'gy_0'=4,'gy_1'=4,'gz'=4] {'gy_0'}, use_global_device_ids=true, to_apply=%region_8.9 | all-reduce | flops 3 | bytes 24 | tf_op jit(solution)/shard_map/psum | solution.py:39
  165.4 8.1 %all-reduce.7 = (f32[]{:T(128)}, f32[]{:T(128)}, f32[]{:T(128)}) all-reduce(f32[]{:T(128)} %get-tuple-element.653, f32[]{:T(128)} %get-tuple-element.654, f32[]{:T(128)} %get-tuple-element.655), channel_id=1, replica_groups=mesh['gx_0'=8,'gx_1'=2,'gy_0'=4,'gy_1'=4,'gz'=4] {'gy_1'}, use_global_device_ids=true, to_apply=%region_9.10 | all-reduce | flops 3 | bytes 24 | tf_op jit(solution)/shard_map/psum | solution.py:39
  173.5 9.2 %all-reduce.5 = (f32[]{:T(128)}, f32[]{:T(128)}, f32[]{:T(128)}) all-reduce(f32[]{:T(128)} %get-tuple-element.647, f32[]{:T(128)} %get-tuple-element.648, f32[]{:T(128)} %get-tuple-element.649), channel_id=1, replica_groups=mesh['gx_0'=8,'gx_1'=2,'gy_0'=4,'gy_1'=4,'gz'=4] {'gz'}, use_global_device_ids=true, to_apply=%region_10.11 | all-reduce | flops 3 | bytes 24 | tf_op jit(solution)/shard_map/psum | solution.py:39
  191.5 8.8 %collective-permute-start.20 = (f32[3,14,3,3]{3,2,1,0:T(4,128)S(1)}, f32[3,14,3,3]{3,2,1,0:T(4,128)S(1)}, u32[]{:S(2)}, u32[]{:S(2)}) collective-permute-start(f32[3,14,3,3]{3,2,1,0:T(4,128)S(1)} %get-tuple-element.694), channel_id=1, source_target_pairs={{0,4},{4,8},{8,12},{12,16},{16,20},{20,24},{24,28},{28,32},{32,36}... | collective-permute-start | bytes 4544 | tf_op jit(solution)/shard_map/ppermute | solution.py:29
  205.7 10.9 %collective-permute-done.21 = f32[3,14,3,3]{3,2,1,0:T(4,128)S(1)} collective-permute-done((f32[3,14,3,3]{3,2,1,0:T(4,128)S(1)}, f32[3,14,3,3]{3,2,1,0:T(4,128)S(1)}, u32[]{:S(2)}, u32[]{:S(2)}) %collective-permute-start.21) | collective-permute-done | bytes 1544 | tf_op jit(solution)/shard_map/ppermute | solution.py:31
  217.1 4.4 %collective-permute-start.23 = (f32[3,14,14,3]{2,1,3,0:T(8,128)S(1)}, f32[3,14,14,3]{2,1,3,0:T(8,128)S(1)}, u32[]{:S(2)}, u32[]{:S(2)}) collective-permute-start(f32[3,14,14,3]{2,1,3,0:T(8,128)S(1)} %pad_maximum_fusion.10), channel_id=1, source_target_pairs={{1,0},{2,1},{3,2},{0,3},{5,4},{6,5},{7,6},{4,7},{9,8},{10,9},{11,1... | collective-permute-start | bytes 21176 | tf_op jit(solution)/shard_map/ppermute | solution.py:31
  223.5 6.1 %collective-permute-done.22 = f32[3,14,14,3]{2,1,3,0:T(8,128)S(1)} collective-permute-done((f32[3,14,14,3]{2,1,3,0:T(8,128)S(1)}, f32[3,14,14,3]{2,1,3,0:T(8,128)S(1)}, u32[]{:S(2)}, u32[]{:S(2)}) %collective-permute-start.22) | collective-permute-done | bytes 7088 | tf_op jit(solution)/shard_map/ppermute | solution.py:29
  230.2 11.1 %while.46 = (s32[]{:T(128)}, f32[3,192]{1,0:T(4,128)S(1)}, s32[14,126]{1,0:T(8,128)S(1)}, f32[14,3,126]{2,1,0:T(4,128)S(1)}, f32[3,1,1,1,192]{4,0,3,2,1:T(4,128)...) while((s32[]{:T(128)}, f32[3,192]{1,0:T(4,128)S(1)}, ...), condition=%wide.region_32.33_spmd.clone, body=%wide.region_28.32_spmd.clone.sunk | while | flops 1500609 | bytes 810071 | solution.py:85
  241.9 16.2 %all-reduce.2 = (f32[]{:T(128)}, f32[]{:T(128)}, f32[]{:T(128)}) all-reduce(f32[]{:T(128)} %get-tuple-element.544, f32[]{:T(128)} %get-tuple-element.545, f32[]{:T(128)} %get-tuple-element.543), channel_id=1, replica_groups=mesh['gx_0'=8,'gx_1'=2,'gy_0'=4,'gy_1'=4,'gz'=4] {'gx_0'}, use_global_device_ids=true, to_apply=%region_34.35 | all-reduce | flops 3 | bytes 24 | tf_op jit(solution)/shard_map/psum | solution.py:39
  261.2 12.1 %all-reduce.8 = (f32[]{:T(128)}, f32[]{:T(128)}, f32[]{:T(128)}) all-reduce(f32[]{:T(128)} %get-tuple-element.656, f32[]{:T(128)} %get-tuple-element.657, f32[]{:T(128)} %get-tuple-element.658), channel_id=1, replica_groups=mesh['gx_0'=8,'gx_1'=2,'gy_0'=4,'gy_1'=4,'gz'=4] {'gy_0'}, use_global_device_ids=true, to_apply=%region_36.37 | all-reduce | flops 3 | bytes 24 | tf_op jit(solution)/shard_map/psum | solution.py:39
  273.3 8.1 %all-reduce.6 = (f32[]{:T(128)}, f32[]{:T(128)}, f32[]{:T(128)}) all-reduce(f32[]{:T(128)} %get-tuple-element.650, f32[]{:T(128)} %get-tuple-element.651, f32[]{:T(128)} %get-tuple-element.652), channel_id=1, replica_groups=mesh['gx_0'=8,'gx_1'=2,'gy_0'=4,'gy_1'=4,'gz'=4] {'gy_1'}, use_global_device_ids=true, to_apply=%region_37.38 | all-reduce | flops 3 | bytes 24 | tf_op jit(solution)/shard_map/psum | solution.py:39
  281.3 9.0 %all-reduce.4 = (f32[]{:T(128)}, f32[]{:T(128)}, f32[]{:T(128)}) all-reduce(f32[]{:T(128)} %get-tuple-element.644, f32[]{:T(128)} %get-tuple-element.645, f32[]{:T(128)} %get-tuple-element.646), channel_id=1, replica_groups=mesh['gx_0'=8,'gx_1'=2,'gy_0'=4,'gy_1'=4,'gz'=4] {'gz'}, use_global_device_ids=true, to_apply=%region_38.39 | all-reduce | flops 3 | bytes 24 | tf_op jit(solution)/shard_map/psum | solution.py:39
  295.9 9.7 %collective-permute-start.26 = (f32[3,14,3,3]{3,2,1,0:T(4,128)S(1)}, f32[3,14,3,3]{3,2,1,0:T(4,128)S(1)}, u32[]{:S(2)}, u32[]{:S(2)}) collective-permute-start(f32[3,14,3,3]{3,2,1,0:T(4,128)S(1)} %get-tuple-element.692), channel_id=1, source_target_pairs={{0,4},{4,8},{8,12},{12,16},{16,20},{20,24},{24,28},{28,32},{32,36}... | collective-permute-start | bytes 4544 | tf_op jit(solution)/shard_map/ppermute | solution.py:29
  308.6 13.5 %collective-permute-done.27 = f32[3,14,3,3]{3,2,1,0:T(4,128)S(1)} collective-permute-done((f32[3,14,3,3]{3,2,1,0:T(4,128)S(1)}, f32[3,14,3,3]{3,2,1,0:T(4,128)S(1)}, u32[]{:S(2)}, u32[]{:S(2)}) %collective-permute-start.27) | collective-permute-done | bytes 1544 | tf_op jit(solution)/shard_map/ppermute | solution.py:31
  333.2 19.5 %while.47 = (s32[]{:T(128)}, f32[3,192]{1,0:T(4,128)S(1)}, f32[14,3,126]{2,1,0:T(4,128)S(1)}, f32[3,1,1,1,192]{4,0,3,2,1:T(4,128)S(1)}, f32[3,192]{1,0:T(4,128)S...) while((s32[]{:T(128)}, f32[3,192]{1,0:T(4,128)S(1)}, ...), condition=%wide.region_47.48_spmd.clone, body=%wide.region_39.47_spmd.clone.sunk | while | flops 4089729 | bytes 2666975 | solution.py:135
  (705 shorter events, 139.4 us)
Async XLA Ops:
  2.2 9.4 %collective-permute-start.6 = (f32[3,3,8,3]{3,2,1,0:T(8,128)S(1)}, f32[3,3,8,3]{3,2,1,0:T(8,128)S(1)}, u32[]{:S(2)}, u32[]{:S(2)}) collective-permute-start(f32[3,3,8,3]{3,2,1,0:T(8,128)S(1)} %get-tuple-element.708), channel_id=1, source_target_pairs={{0,64},{64,128},{128,192},{192,256},{256,320},{320,384},{384,448},... | collective-permute-start | bytes 2600 | tf_op jit(solution)/shard_map/ppermute | solution.py:29
  2.2 9.4 %collective-permute-start.7 = (f32[3,3,8,3]{3,2,1,0:T(8,128)S(1)}, f32[3,3,8,3]{3,2,1,0:T(8,128)S(1)}, u32[]{:S(2)}, u32[]{:S(2)}) collective-permute-start(f32[3,3,8,3]{3,2,1,0:T(8,128)S(1)} %get-tuple-element.709), channel_id=1, source_target_pairs={{64,0},{128,64},{192,128},{256,192},{320,256},{384,320},{448,384},... | collective-permute-start | bytes 2600 | tf_op jit(solution)/shard_map/ppermute | solution.py:31
  6.7 18.1 %collective-permute-start = (f32[4,3,8,3]{3,2,1,0:T(8,128)S(1)}, f32[4,3,8,3]{3,2,1,0:T(8,128)S(1)}, u32[]{:S(2)}, u32[]{:S(2)}) collective-permute-start(f32[4,3,8,3]{3,2,1,0:T(8,128)S(1)} %get-tuple-element.700), channel_id=1, source_target_pairs={{0,64},{64,128},{128,192},{192,256},{256,320},{320,384},{384,448},... | collective-permute-start | bytes 3464 | tf_op jit(solution)/shard_map/ppermute | solution.py:29
  6.7 18.1 %collective-permute-start.1 = (f32[4,3,8,3]{3,2,1,0:T(8,128)S(1)}, f32[4,3,8,3]{3,2,1,0:T(8,128)S(1)}, u32[]{:S(2)}, u32[]{:S(2)}) collective-permute-start(f32[4,3,8,3]{3,2,1,0:T(8,128)S(1)} %get-tuple-element.701), channel_id=1, source_target_pairs={{64,0},{128,64},{192,128},{256,192},{320,256},{384,320},{448,384},... | collective-permute-start | bytes 3464 | tf_op jit(solution)/shard_map/ppermute | solution.py:31
  12.1 25.2 %collective-permute-start.8 = (f32[3,14,3,3]{3,2,1,0:T(4,128)S(1)}, f32[3,14,3,3]{3,2,1,0:T(4,128)S(1)}, u32[]{:S(2)}, u32[]{:S(2)}) collective-permute-start(f32[3,14,3,3]{3,2,1,0:T(4,128)S(1)} %get-tuple-element.698), channel_id=1, source_target_pairs={{0,4},{4,8},{8,12},{12,16},{16,20},{20,24},{24,28},{28,32},{32,36}... | collective-permute-start | bytes 4544 | tf_op jit(solution)/shard_map/ppermute | solution.py:29
  22.9 16.1 %collective-permute-start.9 = (f32[3,14,3,3]{3,2,1,0:T(4,128)S(1)}, f32[3,14,3,3]{3,2,1,0:T(4,128)S(1)}, u32[]{:S(2)}, u32[]{:S(2)}) collective-permute-start(f32[3,14,3,3]{3,2,1,0:T(4,128)S(1)} %get-tuple-element.699), channel_id=1, source_target_pairs={{4,0},{8,4},{12,8},{16,12},{20,16},{24,20},{28,24},{32,28},{36,32}... | collective-permute-start | bytes 4544 | tf_op jit(solution)/shard_map/ppermute | solution.py:31
  25.3 22.7 %collective-permute-start.2 = (f32[4,14,3,3]{3,2,1,0:T(4,128)S(1)}, f32[4,14,3,3]{3,2,1,0:T(4,128)S(1)}, u32[]{:S(2)}, u32[]{:S(2)}) collective-permute-start(f32[4,14,3,3]{3,2,1,0:T(4,128)S(1)} %get-tuple-element.690), channel_id=1, source_target_pairs={{0,4},{4,8},{8,12},{12,16},{16,20},{20,24},{24,28},{28,32},{32,36}... | collective-permute-start | bytes 6056 | tf_op jit(solution)/shard_map/ppermute | solution.py:29
  35.3 16.5 %collective-permute-start.3 = (f32[4,14,3,3]{3,2,1,0:T(4,128)S(1)}, f32[4,14,3,3]{3,2,1,0:T(4,128)S(1)}, u32[]{:S(2)}, u32[]{:S(2)}) collective-permute-start(f32[4,14,3,3]{3,2,1,0:T(4,128)S(1)} %get-tuple-element.691), channel_id=1, source_target_pairs={{4,0},{8,4},{12,8},{16,12},{20,16},{24,20},{28,24},{32,28},{36,32}... | collective-permute-start | bytes 6056 | tf_op jit(solution)/shard_map/ppermute | solution.py:31
  39.6 25.2 %collective-permute-start.11 = (f32[3,14,14,3]{2,1,3,0:T(8,128)S(1)}, f32[3,14,14,3]{2,1,3,0:T(8,128)S(1)}, u32[]{:S(2)}, u32[]{:S(2)}) collective-permute-start(f32[3,14,14,3]{2,1,3,0:T(8,128)S(1)} %pad_maximum_fusion.8), channel_id=1, source_target_pairs={{1,0},{2,1},{3,2},{0,3},{5,4},{6,5},{7,6},{4,7},{9,8},{10,9},{11,1... | collective-permute-start | bytes 21176 | tf_op jit(solution)/shard_map/ppermute | solution.py:31
  46.1 18.7 %collective-permute-start.10 = (f32[3,14,14,3]{2,1,3,0:T(8,128)S(1)}, f32[3,14,14,3]{2,1,3,0:T(8,128)S(1)}, u32[]{:S(2)}, u32[]{:S(2)}) collective-permute-start(f32[3,14,14,3]{2,1,3,0:T(8,128)S(1)} %pad_maximum_fusion.8), channel_id=1, source_target_pairs={{0,1},{1,2},{2,3},{3,0},{4,5},{5,6},{6,7},{7,4},{8,9},{9,10},{10,1... | collective-permute-start | bytes 21176 | tf_op jit(solution)/shard_map/ppermute | solution.py:29
  52.4 13.0 %collective-permute-start.5 = (f32[4,14,14,3]{2,0,3,1:T(4,128)S(1)}, f32[4,14,14,3]{2,0,3,1:T(4,128)S(1)}, u32[]{:S(2)}, u32[]{:S(2)}) collective-permute-start(f32[4,14,14,3]{2,0,3,1:T(4,128)S(1)} %pad_maximum_fusion.7), channel_id=1, source_target_pairs={{1,0},{2,1},{3,2},{0,3},{5,4},{6,5},{7,6},{4,7},{9,8},{10,9},{11,1... | collective-permute-start | bytes 28232 | tf_op jit(solution)/shard_map/ppermute | solution.py:31
  62.9 8.2 %collective-permute-start.4 = (f32[4,14,14,3]{2,0,3,1:T(4,128)S(1)}, f32[4,14,14,3]{2,0,3,1:T(4,128)S(1)}, u32[]{:S(2)}, u32[]{:S(2)}) collective-permute-start(f32[4,14,14,3]{2,0,3,1:T(4,128)S(1)} %pad_maximum_fusion.7), channel_id=1, source_target_pairs={{0,1},{1,2},{2,3},{3,0},{4,5},{5,6},{6,7},{7,4},{8,9},{9,10},{10,1... | collective-permute-start | bytes 28232 | tf_op jit(solution)/shard_map/ppermute | solution.py:29
  88.7 7.3 %collective-permute-start.14 = (f32[3,14,3,3]{3,2,1,0:T(4,128)S(1)}, f32[3,14,3,3]{3,2,1,0:T(4,128)S(1)}, u32[]{:S(2)}, u32[]{:S(2)}) collective-permute-start(f32[3,14,3,3]{3,2,1,0:T(4,128)S(1)} %get-tuple-element.696), channel_id=1, source_target_pairs={{0,4},{4,8},{8,12},{12,16},{16,20},{20,24},{24,28},{28,32},{32,36}... | collective-permute-start | bytes 4544 | tf_op jit(solution)/shard_map/ppermute | solution.py:29
  90.6 12.9 %collective-permute-start.15 = (f32[3,14,3,3]{3,2,1,0:T(4,128)S(1)}, f32[3,14,3,3]{3,2,1,0:T(4,128)S(1)}, u32[]{:S(2)}, u32[]{:S(2)}) collective-permute-start(f32[3,14,3,3]{3,2,1,0:T(4,128)S(1)} %get-tuple-element.697), channel_id=1, source_target_pairs={{4,0},{8,4},{12,8},{16,12},{20,16},{24,20},{28,24},{32,28},{36,32}... | collective-permute-start | bytes 4544 | tf_op jit(solution)/shard_map/ppermute | solution.py:31
  104.1 6.2 %collective-permute-start.17 = (f32[3,14,14,3]{2,1,3,0:T(8,128)S(1)}, f32[3,14,14,3]{2,1,3,0:T(8,128)S(1)}, u32[]{:S(2)}, u32[]{:S(2)}) collective-permute-start(f32[3,14,14,3]{2,1,3,0:T(8,128)S(1)} %pad_maximum_fusion.9), channel_id=1, source_target_pairs={{1,0},{2,1},{3,2},{0,3},{5,4},{6,5},{7,6},{4,7},{9,8},{10,9},{11,1... | collective-permute-start | bytes 21176 | tf_op jit(solution)/shard_map/ppermute | solution.py:31
  106.0 8.0 %collective-permute-start.16 = (f32[3,14,14,3]{2,1,3,0:T(8,128)S(1)}, f32[3,14,14,3]{2,1,3,0:T(8,128)S(1)}, u32[]{:S(2)}, u32[]{:S(2)}) collective-permute-start(f32[3,14,14,3]{2,1,3,0:T(8,128)S(1)} %pad_maximum_fusion.9), channel_id=1, source_target_pairs={{0,1},{1,2},{2,3},{3,0},{4,5},{5,6},{6,7},{7,4},{8,9},{9,10},{10,1... | collective-permute-start | bytes 21176 | tf_op jit(solution)/shard_map/ppermute | solution.py:29
  191.5 13.7 %collective-permute-start.20 = (f32[3,14,3,3]{3,2,1,0:T(4,128)S(1)}, f32[3,14,3,3]{3,2,1,0:T(4,128)S(1)}, u32[]{:S(2)}, u32[]{:S(2)}) collective-permute-start(f32[3,14,3,3]{3,2,1,0:T(4,128)S(1)} %get-tuple-element.694), channel_id=1, source_target_pairs={{0,4},{4,8},{8,12},{12,16},{16,20},{20,24},{24,28},{28,32},{32,36}... | collective-permute-start | bytes 4544 | tf_op jit(solution)/shard_map/ppermute | solution.py:29
  200.3 16.2 %collective-permute-start.21 = (f32[3,14,3,3]{3,2,1,0:T(4,128)S(1)}, f32[3,14,3,3]{3,2,1,0:T(4,128)S(1)}, u32[]{:S(2)}, u32[]{:S(2)}) collective-permute-start(f32[3,14,3,3]{3,2,1,0:T(4,128)S(1)} %get-tuple-element.695), channel_id=1, source_target_pairs={{4,0},{8,4},{12,8},{16,12},{20,16},{24,20},{28,24},{32,28},{36,32}... | collective-permute-start | bytes 4544 | tf_op jit(solution)/shard_map/ppermute | solution.py:31
  217.1 6.4 %collective-permute-start.23 = (f32[3,14,14,3]{2,1,3,0:T(8,128)S(1)}, f32[3,14,14,3]{2,1,3,0:T(8,128)S(1)}, u32[]{:S(2)}, u32[]{:S(2)}) collective-permute-start(f32[3,14,14,3]{2,1,3,0:T(8,128)S(1)} %pad_maximum_fusion.10), channel_id=1, source_target_pairs={{1,0},{2,1},{3,2},{0,3},{5,4},{6,5},{7,6},{4,7},{9,8},{10,9},{11,1... | collective-permute-start | bytes 21176 | tf_op jit(solution)/shard_map/ppermute | solution.py:31
  221.5 8.0 %collective-permute-start.22 = (f32[3,14,14,3]{2,1,3,0:T(8,128)S(1)}, f32[3,14,14,3]{2,1,3,0:T(8,128)S(1)}, u32[]{:S(2)}, u32[]{:S(2)}) collective-permute-start(f32[3,14,14,3]{2,1,3,0:T(8,128)S(1)} %pad_maximum_fusion.10), channel_id=1, source_target_pairs={{0,1},{1,2},{2,3},{3,0},{4,5},{5,6},{6,7},{7,4},{8,9},{9,10},{10,1... | collective-permute-start | bytes 21176 | tf_op jit(solution)/shard_map/ppermute | solution.py:29
  295.9 12.2 %collective-permute-start.26 = (f32[3,14,3,3]{3,2,1,0:T(4,128)S(1)}, f32[3,14,3,3]{3,2,1,0:T(4,128)S(1)}, u32[]{:S(2)}, u32[]{:S(2)}) collective-permute-start(f32[3,14,3,3]{3,2,1,0:T(4,128)S(1)} %get-tuple-element.692), channel_id=1, source_target_pairs={{0,4},{4,8},{8,12},{12,16},{16,20},{20,24},{24,28},{28,32},{32,36}... | collective-permute-start | bytes 4544 | tf_op jit(solution)/shard_map/ppermute | solution.py:29
  305.6 16.5 %collective-permute-start.27 = (f32[3,14,3,3]{3,2,1,0:T(4,128)S(1)}, f32[3,14,3,3]{3,2,1,0:T(4,128)S(1)}, u32[]{:S(2)}, u32[]{:S(2)}) collective-permute-start(f32[3,14,3,3]{3,2,1,0:T(4,128)S(1)} %get-tuple-element.693), channel_id=1, source_target_pairs={{4,0},{8,4},{12,8},{16,12},{20,16},{24,20},{28,24},{32,28},{36,32}... | collective-permute-start | bytes 4544 | tf_op jit(solution)/shard_map/ppermute | solution.py:31
  322.6 7.8 %collective-permute-start.29 = (f32[3,14,14,3]{2,1,3,0:T(8,128)S(1)}, f32[3,14,14,3]{2,1,3,0:T(8,128)S(1)}, u32[]{:S(2)}, u32[]{:S(2)}) collective-permute-start(f32[3,14,14,3]{2,1,3,0:T(8,128)S(1)} %pad_maximum_fusion.11), channel_id=1, source_target_pairs={{1,0},{2,1},{3,2},{0,3},{5,4},{6,5},{7,6},{4,7},{9,8},{10,9},{11,1... | collective-permute-start | bytes 21176 | tf_op jit(solution)/shard_map/ppermute | solution.py:31
  324.5 8.0 %collective-permute-start.28 = (f32[3,14,14,3]{2,1,3,0:T(8,128)S(1)}, f32[3,14,14,3]{2,1,3,0:T(8,128)S(1)}, u32[]{:S(2)}, u32[]{:S(2)}) collective-permute-start(f32[3,14,14,3]{2,1,3,0:T(8,128)S(1)} %pad_maximum_fusion.11), channel_id=1, source_target_pairs={{0,1},{1,2},{2,3},{3,0},{4,5},{5,6},{6,7},{7,4},{8,9},{9,10},{10,1... | collective-permute-start | bytes 21176 | tf_op jit(solution)/shard_map/ppermute | solution.py:29
  (10 other events, 33.8 us)
where the time goes:
time: 355 us; the launch traced here: 354 us
  starting transfers between devices  106 us (30%)
  blocking collectives  105 us (30%)
  waiting for transfers between devices  63.1 us (18%)
  other arithmetic  50.1 us (14%)
  local copies, waits for them, and re-layouts  17.3 us (5%)
  between operations  8.5 us (2%)
  loops' own time  4.17 us (1%)
    psum x10, blocking collectives, one_axis_at_a_time(): return functools.reduce(lax.psum, axes, value)  105 us
    ppermute x15, starting transfers between devices, padded(): lax.ppermute(tail, axis, [(i, (i + 1) % count) for i in range(count)])  54.9 us
    ppermute x15, starting transfers between devices, padded(): lax.ppermute(head, axis, [((i + 1) % count, i) for i in range(count)])  51.5 us
    ppermute x15, waiting for transfers between devices, padded(): lax.ppermute(head, axis, [((i + 1) % count, i) for i in range(count)])  36.7 us
    ppermute x15, waiting for transfers between devices, padded(): lax.ppermute(tail, axis, [(i, (i + 1) % count) for i in range(count)])  26.4 us
    reduce_sum x42, other arithmetic, apply_advance(): jnp.sum(coupling5[None] * displace * along[None] - coupling3[None] * vect...  13.2 us
    mul x42, other arithmetic, tensor_parts(): coupling5 = 3.0 * weight * damp_five * inv_cube * inverse * inverse  7.94 us
  transfers between devices with their start and end apart: 30, of which 16 were waited for; matrix products, arithmetic and copies ran while one was open for 3% of the time, Pallas kernels for 0%

commit v1 on v0

v1 whole, which is shorter than its diff:
```python
import numpy as np

import jax
import jax.numpy as jnp
from jax import lax
from jax.experimental import pallas as pl
from jax.experimental.pallas import tpu as pltpu
from jax.sharding import PartitionSpec as P

LX = 8
LY = 8
DEPTH = 3
CUTOFF = 3
LAYERS = 4
FULL_Z = DEPTH * LAYERS
HALO = 2 * CUTOFF
WIDE = LX + 2 * HALO
ATOMS = LX * LY * DEPTH
ROWS = 24
LANES = 512
BLOCKS = 3
JITTER = 0.4

thole_factor = 0.39
group_scale = 0.5


def within(dx, dy, dz):
    least = sum(max(abs(o) - JITTER, 0.0) ** 2 for o in (dx, dy, dz))
    return least < CUTOFF * CUTOFF


def half_offsets():
    reach = range(-CUTOFF, CUTOFF + 1)
    columns = []
    count = 0
    for dx in range(0, CUTOFF + 1):
        for dy in reach:
            depths = [
                dz
                for dz in reach
                if (dx > 0 or dy > 0 or (dy == 0 and dz > 0)) and within(dx, dy, dz)
            ]
            if depths:
                columns.append((dx, dy, depths, count))
                count += len(depths)
    return columns, count


COLUMNS, OFFSETS = half_offsets()


def may_share_group(dx, dy, dz):
    return dx == 0 and abs(DEPTH * dy + dz) <= 7 and abs(dz) < DEPTH


def lane_iota(rows=ROWS):
    return lax.broadcasted_iota(jnp.int32, (rows, 128), 1)


def shifted(source, field, shift, out, slot):
    if shift == 0:
        for b in range(BLOCKS):
            out[slot, b] = source[field, b]
        return
    keep = lane_iota() < 128 - shift
    turned = [pltpu.roll(source[field, b], 128 - shift, 1) for b in range(BLOCKS + 1)]
    for b in range(BLOCKS):
        out[slot, b] = jnp.where(keep, turned[b], turned[b + 1])


def spread(values, block_rows, total):
    shift = block_rows
    for c in range(3):
        if shift == 0:
            for b in range(BLOCKS):
                total[c, b, 12:36] += values[c, b]
            continue
        keep = lane_iota() >= shift
        turned = [pltpu.roll(values[c, b], shift, 1) for b in range(BLOCKS)]
        for b in range(BLOCKS):
            if b == 0:
                total[c, b, 12:36] += jnp.where(keep, turned[b], 0.0)
            else:
                total[c, b, 12:36] += jnp.where(keep, turned[b], turned[b - 1])


def row_limit(v):
    if v == 0:
        return jnp.ones((8, 128), jnp.float32)
    row = lax.broadcasted_iota(jnp.int32, (8, 128), 0)
    return jnp.where(row < FULL_Z - 8, 1.0, -1.0e3)


def finish(polar_of, own_sum, partner_sum, ring, out):
    for c in range(3):
        for b in range(BLOCKS):
            folded = (
                own_sum[c, b, 0:12]
                + partner_sum[c, b, 15:27]
                + partner_sum[c, b, 27:39]
                + partner_sum[c, b, 3:15]
            )
            value = folded * polar_of(b)
            ring[3:15] = value
            ring[15:27] = value
            ring[27:39] = value
            out[c, b] = ring[12:36]
        out[c, BLOCKS] = jnp.zeros((ROWS, 128), jnp.float32)


def own_lanes(b):
    lane = lax.broadcasted_iota(jnp.int32, (12, 128), 1) + 128 * b
    x = lane // WIDE
    y = lane - x * WIDE
    return (x >= HALO) & (x < HALO + LX) & (y >= HALO) & (y < HALO + LY)


def inner(first, second, inverse_of):
    total = jnp.zeros((12, 128), jnp.float32)
    for b in range(BLOCKS):
        dot = sum(first[c, b, 3:15] * second[c, b, 3:15] for c in range(3))
        total = total + jnp.where(own_lanes(b), dot * inverse_of(b), 0.0)
    return jnp.sum(total)


def apply_pass(vec, spots, spots_far, c3_ref, c5_ref, far, own_sum, partner, partner_sum):
    own_sum[...] = jnp.zeros_like(own_sum)
    partner_sum[...] = jnp.zeros_like(partner_sum)
    for number, (dx, dy, depths, first) in enumerate(COLUMNS):
        shift = dx * WIDE + dy
        for c in range(3):
            shifted(vec, c, shift, far, c)
        partner[...] = jnp.zeros_like(partner)

        def per_block(b, carry):
            for v in range(2):
                rows = pl.ds(3 + 8 * v, 8)
                own = [spots[c, b, rows, :] for c in range(3)]
                own_u = [vec[c, b, rows, :] for c in range(3)]
                acc = [own_sum[c, b, pl.ds(8 * v, 8), :] for c in range(3)]
                for n, dz in enumerate(depths):
                    far_rows = pl.ds(3 + dz + 8 * v, 8)
                    d = [spots_far[number, c, b, far_rows, :] - own[c] for c in range(3)]
                    far_u = [far[c, b, far_rows, :] for c in range(3)]
                    c3 = c3_ref[first + n, b, pl.ds(8 * v, 8), :]
                    c5 = c5_ref[first + n, b, pl.ds(8 * v, 8), :]
                    along_far = c5 * (d[0] * far_u[0] + d[1] * far_u[1] + d[2] * far_u[2])
                    along_own = c5 * (d[0] * own_u[0] + d[1] * own_u[1] + d[2] * own_u[2])
                    for c in range(3):
                        acc[c] = acc[c] + (along_far * d[c] - c3 * far_u[c])
                        partner[c, b, far_rows, :] += along_own * d[c] - c3 * own_u[c]
                for c in range(3):
                    own_sum[c, b, pl.ds(8 * v, 8), :] = acc[c]
            return carry

        lax.fori_loop(0, BLOCKS, per_block, 0)
        spread(partner, shift, partner_sum)


def first_kernel(
    base_ref, c3_ref, c5_ref, spots_far, u1_ref, u2_ref, moment_ref,
    fields, far, own_sum, partner, partner_sum, ring, vec, vec_b,
):
    for b in range(BLOCKS + 1):
        lanes = slice(128 * b, 128 * b + 128)
        for f in range(3):
            fields[f, b] = base_ref[f, :, lanes]
            vec[f, b] = base_ref[4 + f, :, lanes]
        polar = base_ref[3, :, lanes]
        fields[3, b] = (thole_factor**0.5) * lax.rsqrt(polar)
        fields[4, b] = base_ref[7, :, lanes]
        fields[5, b] = polar
    polar_of = lambda b: fields[5, b, 3:15]
    inverse_of = lambda b: 1.0 / fields[5, b, 3:15]

    own_sum[...] = jnp.zeros_like(own_sum)
    partner_sum[...] = jnp.zeros_like(partner_sum)
    for number, (dx, dy, depths, first) in enumerate(COLUMNS):
        shift = dx * WIDE + dy
        for c in range(3):
            shifted(fields, c, shift, spots_far.at[number], c)
            shifted(vec, c, shift, far, c)
        shifted(fields, 3, shift, far, 3)
        if dx == 0:
            shifted(fields, 4, shift, far, 4)
        partner[...] = jnp.zeros_like(partner)

        def per_block(b, carry):
            for v in range(2):
                rows = pl.ds(3 + 8 * v, 8)
                own = [fields[c, b, rows, :] for c in range(3)]
                root = fields[3, b, rows, :]
                own_u = [vec[c, b, rows, :] for c in range(3)]
                limit = row_limit(v)
                acc = [own_sum[c, b, pl.ds(8 * v, 8), :] for c in range(3)]
                for n, dz in enumerate(depths):
                    far_rows = pl.ds(3 + dz + 8 * v, 8)
                    d = [spots_far[number, c, b, far_rows, :] - own[c] for c in range(3)]
                    far_u = [far[c, b, far_rows, :] for c in range(3)]
                    s = d[0] * d[0] + d[1] * d[1] + d[2] * d[2]
                    inv = lax.rsqrt(s)
                    inv2 = inv * inv
                    inv3 = inv2 * inv
                    x = (s * s * inv) * (root * far[3, b, far_rows, :])
                    e = jnp.exp(-x)
                    l3 = 1.0 - e
                    l5 = l3 - x * e
                    cut = jnp.maximum(limit - s * (1.0 / (CUTOFF * CUTOFF)), 0.0)
                    weight = cut * cut * inv3
                    if may_share_group(dx, dy, dz):
                        same = fields[4, b, rows, :] == far[4, b, far_rows, :]
                        weight = jnp.where(same, group_scale * weight, weight)
                    c3 = weight * l3
                    c5 = (3.0 * weight) * (inv2 * l5)
                    c3_ref[first + n, b, pl.ds(8 * v, 8), :] = c3
                    c5_ref[first + n, b, pl.ds(8 * v, 8), :] = c5
                    along_far = c5 * (d[0] * far_u[0] + d[1] * far_u[1] + d[2] * far_u[2])
                    along_own = c5 * (d[0] * own_u[0] + d[1] * own_u[1] + d[2] * own_u[2])
                    for c in range(3):
                        acc[c] = acc[c] + (along_far * d[c] - c3 * far_u[c])
                        partner[c, b, far_rows, :] += along_own * d[c] - c3 * own_u[c]
                for c in range(3):
                    own_sum[c, b, pl.ds(8 * v, 8), :] = acc[c]
            return carry

        lax.fori_loop(0, BLOCKS, per_block, 0)
        spread(partner, shift, partner_sum)
    finish(polar_of, own_sum, partner_sum, ring, vec_b)
    moments = [inner(vec, vec, inverse_of), inner(vec, vec_b, inverse_of), inner(vec_b, vec_b, inverse_of)]
    for c in range(3):
        for b in range(BLOCKS + 1):
            u1_ref[c, :, 128 * b : 128 * b + 128] = vec_b[c, b]
    apply_pass(vec_b, fields, spots_far, c3_ref, c5_ref, far, own_sum, partner, partner_sum)
    finish(polar_of, own_sum, partner_sum, ring, vec)
    moments += [inner(vec_b, vec, inverse_of), inner(vec, vec, inverse_of)]
    for c in range(3):
        for b in range(BLOCKS):
            u2_ref[c, :, 128 * b : 128 * b + 128] = vec[c, b, 3:15]
    lane = lax.broadcasted_iota(jnp.int32, (1, 128), 1)
    row = jnp.zeros((1, 128), jnp.float32)
    for n, value in enumerate(moments):
        row = jnp.where(lane == n, value, row)
    moment_ref[...] = row


def second_kernel(
    base_ref, c3_ref, c5_ref, spots_far, u2_ref, moment_in, u3_ref, moment_ref,
    fields, far, own_sum, partner, partner_sum, ring, vec, vec_b,
):
    for b in range(BLOCKS + 1):
        lanes = slice(128 * b, 128 * b + 128)
        for f in range(3):
            fields[f, b] = base_ref[f, :, lanes]
            vec[f, b] = u2_ref[f, :, lanes]
        fields[3, b] = base_ref[3, :, lanes]
    polar_of = lambda b: fields[3, b, 3:15]
    inverse_of = lambda b: 1.0 / fields[3, b, 3:15]
    apply_pass(vec, fields, spots_far, c3_ref, c5_ref, far, own_sum, partner, partner_sum)
    finish(polar_of, own_sum, partner_sum, ring, vec_b)
    for c in range(3):
        for b in range(BLOCKS + 1):
            u3_ref[c, :, 128 * b : 128 * b + 128] = vec_b[c, b]
    lane = lax.broadcasted_iota(jnp.int32, (1, 128), 1)
    moment_ref[...] = jnp.where(lane == 5, inner(vec, vec_b, inverse_of), moment_in[...])


def gradient_kernel(moment_ref, own_ref, far_ref, out_ref, energy_ref):
    total = jnp.sum(moment_ref[...], axis=0, keepdims=True)
    lane = lax.broadcasted_iota(jnp.int32, (1, 128), 1)

    def pick(n):
        return jnp.sum(jnp.where(lane == n, total, 0.0), axis=1, keepdims=True)

    m0, m1, m2, m3, m4, m5 = (pick(n) for n in range(6))
    g = m2 / (m2 - m3)
    rest = 1.0 - g
    rz1 = rest * rest * m2 + 2.0 * g * rest * m3 + g * g * m4
    a = rest + rz1 / m2
    curve = a * a * (m2 - m3) + 2.0 * a * g * (m3 - m4) + g * g * (m4 - m5)
    g1 = rz1 / curve
    k1 = g + g1 * a
    k2 = g1 * g
    energy_ref[...] = -(m0 + k1 * m1 + k2 * m2)
    far_k1 = jnp.broadcast_to(k1, (1, 128))
    far_k2 = jnp.broadcast_to(k2, (1, 128))

    def plane(x, carry):
        far = []
        for n in range(2 * CUTOFF + 1):
            block = far_ref[x + n]
            spot = [block[c : c + 1] for c in range(5)]
            u = [[block[5 + 3 * q + c : 6 + 3 * q + c] for c in range(3)] for q in range(4)]
            dip = [u[0][c] + far_k1 * u[1][c] + far_k2 * u[2][c] for c in range(3)]
            adj = [u[0][c] + u[1][c] + far_k1 * u[2][c] + far_k2 * u[3][c] for c in range(3)]
            far.append((spot, dip, adj))
        for t in range(LY * DEPTH // 8):
            start = pl.multiple_of(x * (LY * DEPTH) + 8 * t, 8)
            own_block = own_ref[pl.ds(start, 8), :]

            def own_field(n):
                return jnp.broadcast_to(own_block[:, n : n + 1], (8, 128))

            spot_i = [own_field(c) for c in range(5)]
            u = [[own_field(5 + 3 * q + c) for c in range(3)] for q in range(4)]
            dip_i = [u[0][c] + k1 * u[1][c] + k2 * u[2][c] for c in range(3)]
            adj_i = [u[0][c] + u[1][c] + k1 * u[2][c] + k2 * u[3][c] for c in range(3)]
            acc = [jnp.zeros((8, 128), jnp.float32) for _ in range(3)]
            for n in range(2 * CUTOFF + 1):
                spot, dip, adj = far[n]
                d = [spot[c] - spot_i[c] for c in range(3)]
                s = d[0] * d[0] + d[1] * d[1] + d[2] * d[2]
                if n == CUTOFF:
                    own_atom = s == 0.0
                    s = jnp.where(own_atom, 1.0, s)
                inv = lax.rsqrt(s)
                inv2 = inv * inv
                x_damp = (s * s * inv) * (spot_i[3] * spot[3])
                xe = x_damp * jnp.exp(-x_damp)
                e = jnp.exp(-x_damp)
                l3 = 1.0 - e
                l5 = l3 - xe
                cut = jnp.maximum(1.0 - s * (1.0 / (CUTOFF * CUTOFF)), 0.0)
                scale = inv2 * inv
                if n == CUTOFF:
                    scale = jnp.where(spot[4] == spot_i[4], group_scale * scale, scale)
                    scale = jnp.where(own_atom, 0.0, scale)
                ratio = cut * inv2
                scale = scale * cut
                scale5 = 3.0 * scale * inv2
                c5 = scale5 * cut * l5
                slope3 = scale * ((-4.0 / (CUTOFF * CUTOFF)) * l3 - 3.0 * ratio * l5)
                slope5 = scale5 * (
                    (-4.0 / (CUTOFF * CUTOFF)) * l5 + ratio * (3.0 * x_damp * xe - 5.0 * l5)
                )
                own_dip = d[0] * dip_i[0] + d[1] * dip_i[1] + d[2] * dip_i[2]
                own_adj = d[0] * adj_i[0] + d[1] * adj_i[1] + d[2] * adj_i[2]
                far_dip = d[0] * dip[0] + d[1] * dip[1] + d[2] * dip[2]
                far_adj = d[0] * adj[0] + d[1] * adj[1] + d[2] * adj[2]
                cross = (
                    dip_i[0] * adj[0] + dip_i[1] * adj[1] + dip_i[2] * adj[2]
                    + adj_i[0] * dip[0] + adj_i[1] * dip[1] + adj_i[2] * dip[2]
                )
                radial = slope5 * (own_dip * far_adj + own_adj * far_dip) - slope3 * cross
                p1, p2, p3, p4 = c5 * own_dip, c5 * far_adj, c5 * own_adj, c5 * far_dip
                for c in range(3):
                    acc[c] = acc[c] + (
                        radial * d[c] + p1 * adj[c] + p2 * dip_i[c] + p3 * dip[c] + p4 * adj_i[c]
                    )
            lanes = lax.broadcasted_iota(jnp.int32, (8, 128), 1)
            result = jnp.zeros((8, 128), jnp.float32)
            for c in range(3):
                result = jnp.where(lanes == c, dip_i[c], result)
                force = -0.5 * jnp.sum(acc[c], axis=1, keepdims=True)
                result = jnp.where(lanes == 3 + c, force, result)
            out_ref[pl.ds(start, 8), :] = result
        return carry

    lax.fori_loop(0, LX, plane, 0)


def vmem_specs(count):
    return [pl.BlockSpec(memory_space=pltpu.VMEM)] * count


F32 = jnp.float32
SCRATCH = [
    pltpu.VMEM((6, BLOCKS + 1, ROWS, 128), F32),
    pltpu.VMEM((5, BLOCKS, ROWS, 128), F32),
    pltpu.VMEM((3, BLOCKS, 16, 128), F32),
    pltpu.VMEM((3, BLOCKS, ROWS, 128), F32),
    pltpu.VMEM((3, BLOCKS, 48, 128), F32),
    pltpu.VMEM((48, 128), F32),
    pltpu.VMEM((3, BLOCKS + 1, ROWS, 128), F32),
    pltpu.VMEM((3, BLOCKS + 1, ROWS, 128), F32),
]
COUPLING = jax.ShapeDtypeStruct((OFFSETS, BLOCKS, 16, 128), F32)
PARAMS = pltpu.CompilerParams(vmem_limit_bytes=40 * 1024 * 1024)


def run_first(base):
    outs = (
        COUPLING,
        COUPLING,
        jax.ShapeDtypeStruct((len(COLUMNS), 3, BLOCKS, ROWS, 128), F32),
        jax.ShapeDtypeStruct((3, ROWS, LANES), F32),
        jax.ShapeDtypeStruct((3, FULL_Z, 128 * BLOCKS), F32),
        jax.ShapeDtypeStruct((1, 128), F32),
    )
    return pl.pallas_call(
        first_kernel,
        out_shape=outs,
        in_specs=vmem_specs(1),
        out_specs=tuple(vmem_specs(len(outs))),
        scratch_shapes=SCRATCH,
        compiler_params=PARAMS,
    )(base)


def run_second(base, c3, c5, spots_far, u2, moments):
    outs = (jax.ShapeDtypeStruct((3, ROWS, LANES), F32), jax.ShapeDtypeStruct((1, 128), F32))
    return pl.pallas_call(
        second_kernel,
        out_shape=outs,
        in_specs=vmem_specs(6),
        out_specs=tuple(vmem_specs(2)),
        scratch_shapes=SCRATCH,
        compiler_params=PARAMS,
    )(base, c3, c5, spots_far, u2, moments)


def run_gradient(moments, own, far):
    return pl.pallas_call(
        gradient_kernel,
        out_shape=(
            jax.ShapeDtypeStruct((ATOMS, 128), F32),
            jax.ShapeDtypeStruct((1, 1), F32),
        ),
        in_specs=vmem_specs(3),
        out_specs=tuple(vmem_specs(2)),
        compiler_params=PARAMS,
    )(moments, own, far)


def both_sides(low, high, axis):
    count = lax.axis_size(axis)
    below = lax.ppermute(high, axis, [(i, (i + 1) % count) for i in range(count)])
    above = lax.ppermute(low, axis, [((i + 1) % count, i) for i in range(count)])
    return below, above


def widen(lattice):
    lead = lattice.shape[:-2]
    low = lattice[..., :HALO].reshape(*lead, LX * HALO)
    high = lattice[..., LY - HALO :].reshape(*lead, LX * HALO)
    below, above = both_sides(low, high, "gy")
    along_y = jnp.concatenate(
        [below.reshape(*lead, LX, HALO), lattice, above.reshape(*lead, LX, HALO)], axis=-1
    ).reshape(*lead, LX * WIDE)
    below, above = both_sides(
        along_y[..., : HALO * WIDE], along_y[..., (LX - HALO) * WIDE :], "gx"
    )
    flat = jnp.concatenate([below, along_y, above], axis=-1)
    flat = jnp.pad(flat, [(0, 0)] * len(lead) + [(0, LANES - WIDE * WIDE)])
    return jnp.concatenate([flat[:, FULL_Z - CUTOFF :], flat, flat[:, : ROWS - FULL_Z - CUTOFF]], axis=1)


def frame_constants():
    lane = np.arange(LANES)
    x, y = lane // WIDE, lane % WIDE
    row = np.arange(ROWS)
    full = np.zeros((8, ROWS, LANES), np.float32)
    full[0] = (x - HALO)[None, :]
    full[1] = (y - HALO)[None, :]
    full[2] = (row - CUTOFF)[:, None]
    full[3] = np.where(lane >= WIDE * WIDE, 0.05, 0.0)[None, :]
    domain = (x + 2) // LX * 8 + (y + 2) // LY
    layer = (row - CUTOFF) % FULL_Z // DEPTH
    full[7] = 64.0 * (domain[None, :] * LAYERS + layer[:, None])
    return full


def on_device(positions, polarizability, direct_field, groups):
    site = np.arange(ATOMS)
    lattice = np.stack([site // (LY * DEPTH), site // DEPTH % LY, site % DEPTH]).astype(np.float32)
    polar = polarizability.reshape(1, ATOMS)
    start = polar * direct_field.reshape(3, ATOMS)
    packed = jnp.concatenate(
        [positions.reshape(3, ATOMS) - lattice, polar, start, groups.reshape(1, ATOMS).astype(F32)]
    )
    column = packed.reshape(8, LX * LY, DEPTH).transpose(0, 2, 1)
    layer = lax.axis_index("gz")
    copies = jnp.broadcast_to(column[None], (LAYERS, *column.shape))
    column = lax.all_to_all(copies, "gz", 0, 0).transpose(1, 0, 2, 3)
    base = widen(column.reshape(8, FULL_Z, LX, LY)) + frame_constants()
    c3, c5, spots_far, u1, u2, moments = run_first(base)
    own_u2 = u2[..., HALO * WIDE : (HALO + LX) * WIDE].reshape(3, FULL_Z, LX, WIDE)
    u2_wide = widen(own_u2[..., HALO : HALO + LY])
    u3, moments = run_second(base, c3, c5, spots_far, u2_wide, moments)
    for axis in ("gx", "gy"):
        count = lax.axis_size(axis)
        copies = jnp.broadcast_to(moments[None], (count, 1, 128))
        moments = lax.all_to_all(copies, axis, 0, 0).reshape(count, 128)
        if axis == "gx":
            moments = jnp.sum(moments, axis=0, keepdims=True)
    root = (thole_factor**0.5) * lax.rsqrt(base[3:4])
    everything = jnp.concatenate([base[:3], root, base[7:8], base[4:7], u1, u2_wide, u3])
    nearby = lax.dynamic_slice_in_dim(everything, layer * DEPTH, DEPTH + 2 * CUTOFF, axis=1)
    nearby = nearby[..., : WIDE * WIDE].reshape(-1, DEPTH + 2 * CUTOFF, WIDE, WIDE)
    inside = slice(HALO - CUTOFF, HALO + LX + CUTOFF)
    nearby = nearby[:, :, inside, inside]
    own = nearby[:, CUTOFF:-CUTOFF, CUTOFF:-CUTOFF, CUTOFF:-CUTOFF]
    own = own.transpose(2, 3, 1, 0).reshape(ATOMS, -1)
    far = nearby.transpose(2, 0, 3, 1).reshape(LX + 2 * CUTOFF, nearby.shape[0], -1)
    far = jnp.pad(far, ((0, 0), (0, 0), (0, 128 - far.shape[-1])), constant_values=1.0e3)
    out, energy = run_gradient(moments, own, far)
    out = out[:, :6].T
    devices = lax.axis_size("gx") * lax.axis_size("gy") * lax.axis_size("gz")
    return (
        out[:3].reshape(3, 1, 1, 1, ATOMS),
        out[3:].reshape(3, 1, 1, 1, ATOMS),
        (energy / (2.0 * ATOMS * devices)).reshape(()),
    )


def solution(mesh):
    along = ("gx", "gy", "gz", None)
    return jax.shard_map(
        on_device,
        mesh=mesh,
        in_specs=(P(None, *along), P(*along), P(None, *along), P(*along)),
        out_specs=(P(None, *along), P(None, *along), P()),
        check_vma=False,
    )
```

time: 355 us -> 168 us (0.47)
  blocking collectives: 105 us -> 12.7 us
  starting transfers between devices: 106 us -> 45.8 us
  other arithmetic: 50.1 us -> 6.39 us
  Pallas kernels: 0 us -> 28.5 us
  waiting for transfers between devices: 63.1 us -> 49.2 us
  between operations: 8.5 us -> 2.8 us
  loops' own time: 4.17 us -> 0 us
  local copies, waits for them, and re-layouts: 17.3 us -> 21.4 us
    psum x10 -> x0, blocking collectives: 105 us -> none  [one_axis_at_a_time(): return functools.reduce(lax.psum, axes, value)]
    ppermute x30 -> x8, starting transfers between devices: 106 us -> 24.8 us  [the longest x4 12.8 us: both_sides(): lax.ppermute(high, axis, [(i, (i + 1) % count) for i in range(count)])]
    ppermute x30 -> x8, waiting for transfers between devices: 63.1 us -> 31.2 us  [the longest x4 20.9 us: both_sides(): lax.ppermute(low, axis, [((i + 1) % count, i) for i in range(count)])]
    reduce_sum x114 -> x1, other arithmetic: 31.1 us -> 0.02 us  [on_device(): moments = jnp.sum(moments, axis=0, keepdims=True)]
    pallas_call x0 -> x3, Pallas kernels: none -> 28.5 us  [the longest x1 17.3 us: run_first(): pl.pallas_call(first_kernel, out_shape=outs, in_specs=vmem_specs(1), out_...]
    all_to_all x0 -> x2, starting transfers between devices: none -> 21 us  [on_device(): moments = lax.all_to_all(copies, axis, 0, 0).reshape(count, 128)]
    all_to_all x0 -> x2, waiting for transfers between devices: none -> 18 us  [on_device(): moments = lax.all_to_all(copies, axis, 0, 0).reshape(count, 128)]
    mul x72 -> x1, other arithmetic: 14.4 us -> 0.01 us  [on_device(): start = polar * direct_field.reshape(3, ATOMS)]
  transfers between devices with their start and end apart: 30 -> 10, of which waited for: 16 -> 7; matrix products, arithmetic and copies ran while one was open for 3% -> 4% of each run, Pallas kernels for 0% -> 0%
where the time goes in v1:
time: 168 us; the launch traced here: 167 us
  waiting for transfers between devices  49.2 us (29%)
  starting transfers between devices  45.8 us (27%)
  Pallas kernels  28.5 us (17%)
  local copies, waits for them, and re-layouts  21.4 us (13%)
  blocking collectives  12.7 us (8%)
  other arithmetic  6.39 us (4%)
  between operations  2.8 us (2%)
    all_to_all x2, starting transfers between devices, on_device(): moments = lax.all_to_all(copies, axis, 0, 0).reshape(count, 128)  21 us
    ppermute x4, waiting for transfers between devices, both_sides(): lax.ppermute(low, axis, [((i + 1) % count, i) for i in range(count)])  20.9 us
    all_to_all x2, waiting for transfers between devices, on_device(): moments = lax.all_to_all(copies, axis, 0, 0).reshape(count, 128)  18 us
    pallas_call x1, Pallas kernels, run_first(): pl.pallas_call(first_kernel, out_shape=outs, in_specs=vmem_specs(1), out_...  17.3 us
    ppermute x4, starting transfers between devices, both_sides(): lax.ppermute(high, axis, [(i, (i + 1) % count) for i in range(count)])  12.8 us
    all_to_all x1, blocking collectives, on_device(): column = lax.all_to_all(copies, 'gz', 0, 0).transpose(1, 0, 2, 3)  12.7 us
    ppermute x4, starting transfers between devices, both_sides(): lax.ppermute(low, axis, [((i + 1) % count, i) for i in range(count)])  12 us
    unnamed x22, local copies, waits for them, and re-layouts  10.6 us
  transfers between devices with their start and end apart: 10, of which 7 were waited for; matrix products, arithmetic and copies ran while one was open for 4% of the time, Pallas kernels for 0%

profile of v1, /device:TPU:6, one launch (start us, length us, event | category | flops | bytes accessed | tf_op | source)
XLA Modules:
  0.0 166.7 jit_solution(3990300175896148304)
XLA Ops:
  3.9 1.3 reduce.13
  6.5 12.7 %all_to_all.15 = f32[4,1,1536]{2,1,0:T(1,128)S(1)} all-to-all(f32[4,1,1536]{2,1,0:T(1,128)S(1)} %reshape.149), channel_id=1, replica_groups=mesh['gx'=16,'gy'=16,'gz'=4] {'gz'}, dimensions={0} | all-to-all | bytes 49152 | tf_op jit(solution)/shard_map/all_to_all | solution.py:474
  21.4 10.8 %collective-permute-start = (f32[8,12,48]{1,0,2:T(8,128)S(1)}, f32[8,12,48]{1,0,2:T(8,128)S(1)}, u32[]{:S(2)}, u32[]{:S(2)}) collective-permute-start(f32[8,12,48]{1,0,2:T(8,128)S(1)} %bitcast.51), channel_id=1, source_target_pairs={{0,4},{4,8},{8,12},{12,16},{16,20},{20,24},{24,28},{28,32},{32,36}... | collective-permute-start | bytes 55304 | tf_op jit(solution)/shard_map/ppermute | solution.py:427
  32.8 1.9 %collective-permute-start.1 = (f32[8,12,48]{1,0,2:T(8,128)S(1)}, f32[8,12,48]{1,0,2:T(8,128)S(1)}, u32[]{:S(2)}, u32[]{:S(2)}) collective-permute-start(f32[8,12,48]{1,0,2:T(8,128)S(1)} %bitcast.53), channel_id=1, source_target_pairs={{4,0},{8,4},{12,8},{16,12},{20,16},{24,20},{28,24},{32,28},{36,32}... | collective-permute-start | bytes 55304 | tf_op jit(solution)/shard_map/ppermute | solution.py:428
  34.7 7.5 %collective-permute-done = f32[8,12,48]{1,0,2:T(8,128)S(1)} collective-permute-done((f32[8,12,48]{1,0,2:T(8,128)S(1)}, f32[8,12,48]{1,0,2:T(8,128)S(1)}, u32[]{:S(2)}, u32[]{:S(2)}) %collective-permute-start) | collective-permute-done | bytes 18464 | tf_op jit(solution)/shard_map/ppermute | solution.py:427
  42.8 15.5 %collective-permute-done.1 = f32[8,12,48]{1,0,2:T(8,128)S(1)} collective-permute-done((f32[8,12,48]{1,0,2:T(8,128)S(1)}, f32[8,12,48]{1,0,2:T(8,128)S(1)}, u32[]{:S(2)}, u32[]{:S(2)}) %collective-permute-start.1) | collective-permute-done | bytes 18464 | tf_op jit(solution)/shard_map/ppermute | solution.py:428
  59.5 3.0 %collective-permute-start.3 = (f32[8,12,120]{2,1,0:T(8,128)S(1)}, f32[8,12,120]{2,1,0:T(8,128)S(1)}, u32[]{:S(2)}, u32[]{:S(2)}) collective-permute-start(f32[8,12,120]{2,1,0:T(8,128)S(1)} %get-tuple-element.45), channel_id=1, source_target_pairs={{64,0},{128,64},{192,128},{256,192},{320,256},{384,320},{448,384},... | collective-permute-start | bytes 138248 | tf_op jit(solution)/shard_map/ppermute | solution.py:428
  62.5 1.9 %collective-permute-done.2 = f32[8,12,120]{2,1,0:T(8,128)S(1)} collective-permute-done((f32[8,12,120]{2,1,0:T(8,128)S(1)}, f32[8,12,120]{2,1,0:T(8,128)S(1)}, u32[]{:S(2)}, u32[]{:S(2)}) %collective-permute-start.2) | collective-permute-done | bytes 46112 | tf_op jit(solution)/shard_map/ppermute | solution.py:427
  64.8 17.3 %shard_map.85 = (f32[89,3,16,128]{3,2,1,0:T(8,128)S(1)}, f32[89,3,16,128]{3,2,1,0:T(8,128)S(1)}, f32[19,3,3,24,128]{4,3,2,1,0:T(8,128)S(1)}, f32[3,24,512]{2,1,0...) custom-call(f32[8,24,512]{2,1,0:T(8,128)S(1)} %maximum_add_fusion.base_ref), custom_call_target="tpu_custom_call" | custom-call | tf_op jit(solution)/shard_map/pallas_call | solution.py:390
  82.0 1.4 copy-done
  83.4 1.3 copy-done.2
  85.9 1.9 %collective-permute-start.4 = (f32[3,12,48]{2,1,0:T(8,128)S(1)}, f32[3,12,48]{2,1,0:T(8,128)S(1)}, u32[]{:S(2)}, u32[]{:S(2)}) collective-permute-start(f32[3,12,48]{2,1,0:T(8,128)S(1)} %reshape.115), channel_id=1, source_target_pairs={{0,4},{4,8},{8,12},{12,16},{16,20},{20,24},{24,28},{28,32},{32,36}... | collective-permute-start | bytes 20744 | tf_op jit(solution)/shard_map/ppermute | solution.py:427
  87.9 4.1 %collective-permute-start.5 = (f32[3,12,48]{2,1,0:T(8,128)S(1)}, f32[3,12,48]{2,1,0:T(8,128)S(1)}, u32[]{:S(2)}, u32[]{:S(2)}) collective-permute-start(f32[3,12,48]{2,1,0:T(8,128)S(1)} %reshape.117), channel_id=1, source_target_pairs={{4,0},{8,4},{12,8},{16,12},{20,16},{24,20},{28,24},{32,28},{36,32}... | collective-permute-start | bytes 20744 | tf_op jit(solution)/shard_map/ppermute | solution.py:428
  94.2 5.5 %collective-permute-done.5 = f32[3,12,48]{2,1,0:T(8,128)S(1)} collective-permute-done((f32[3,12,48]{2,1,0:T(8,128)S(1)}, f32[3,12,48]{2,1,0:T(8,128)S(1)}, u32[]{:S(2)}, u32[]{:S(2)}) %collective-permute-start.5) | collective-permute-done | bytes 6944 | tf_op jit(solution)/shard_map/ppermute | solution.py:428
  100.1 3.0 %collective-permute-start.7 = (f32[3,12,120]{2,1,0:T(8,128)S(1)}, f32[3,12,120]{2,1,0:T(8,128)S(1)}, u32[]{:S(2)}, u32[]{:S(2)}) collective-permute-start(f32[3,12,120]{2,1,0:T(8,128)S(1)} %get-tuple-element.49), channel_id=1, source_target_pairs={{64,0},{128,64},{192,128},{256,192},{320,256},{384,320},{448,384},... | collective-permute-start | bytes 51848 | tf_op jit(solution)/shard_map/ppermute | solution.py:428
  105.4 1.6 copy-done.1
  107.0 1.6 copy-done.3
  108.6 7.2 %shard_map.86 = (f32[3,24,512]{2,1,0:T(8,128)S(1)}, f32[1,128]{1,0:T(1,128)S(1)}) custom-call(f32[8,24,512]{2,1,0:T(8,128)S(1)} %maximum_add_fusion.base_ref, f32[89,3,16,128]{3,2,1,0:T(8,128)S(1)} %get-tuple-element.13.c3_ref, f32[89,3,16,128]{3,2,1,0:T(8,128)S(1)} %copy-done.1, f32[19,3,3,24,128]{4,3,2,1,0:T(8,128)S(1)} %copy-done.3, ...), custom_call_target="tpu_custom_call" | custom-call | tf_op jit(solution)/shard_map/pallas_call | solution.py:402
  117.4 7.4 %all-to-all-start.1 = ((f32[16,1,128]{2,1,0:T(1,128)}), f32[16,1,128]{2,1,0:T(1,128)S(1)}, u32[]{:S(2)}, u32[]{:S(2)}) async-start(f32[16,1,128]{2,1,0:T(1,128)} %broadcast_in_dim.10), calls=%async_computation.1 | async-start | bytes 16384 | tf_op jit(solution)/shard_map/all_to_all | solution.py:483
  125.2 7.2 %all-to-all-done.1 = f32[16,1,128]{2,1,0:T(1,128)S(1)} async-done(((f32[16,1,128]{2,1,0:T(1,128)}), f32[16,1,128]{2,1,0:T(1,128)S(1)}, u32[]{:S(2)}, u32[]{:S(2)}) %all-to-all-start.1) | async-done | bytes 8224 | tf_op jit(solution)/shard_map/all_to_all | solution.py:483
  133.0 13.6 %all-to-all-start.2 = ((f32[16,1,128]{2,1,0:T(1,128)}), f32[16,1,128]{2,1,0:T(1,128)S(1)}, u32[]{:S(2)}, u32[]{:S(2)}) async-start(f32[16,1,128]{2,1,0:T(1,128)} %broadcast_in_dim.22), calls=%async_computation.2 | async-start | bytes 16384 | tf_op jit(solution)/shard_map/all_to_all | solution.py:483
  146.8 1.1 copy.76
  148.7 10.8 %all-to-all-done.2 = f32[16,1,128]{2,1,0:T(1,128)S(1)} async-done(((f32[16,1,128]{2,1,0:T(1,128)}), f32[16,1,128]{2,1,0:T(1,128)S(1)}, u32[]{:S(2)}, u32[]{:S(2)}) %all-to-all-start.2) | async-done | bytes 8224 | tf_op jit(solution)/shard_map/all_to_all | solution.py:483
  159.5 4.0 %shard_map.87 = (f32[192,128]{1,0:T(8,128)S(1)}, f32[1,1]{1,0:T(1,128)}) custom-call(f32[16,128]{1,0:T(8,128)S(1)} %bitcast.46, f32[192,17]{1,0:T(8,128)S(1)} %reshape.122.own_ref, f32[14,17,128]{2,1,0:T(8,128)S(1)} %pad.14.far_ref), custom_call_target="tpu_custom_call" | custom-call | tf_op jit(solution)/shard_map/pallas_call | solution.py:413
  (84 shorter events, 20.2 us)
Async XLA Ops:
  21.4 20.8 %collective-permute-start = (f32[8,12,48]{1,0,2:T(8,128)S(1)}, f32[8,12,48]{1,0,2:T(8,128)S(1)}, u32[]{:S(2)}, u32[]{:S(2)}) collective-permute-start(f32[8,12,48]{1,0,2:T(8,128)S(1)} %bitcast.51), channel_id=1, source_target_pairs={{0,4},{4,8},{8,12},{12,16},{16,20},{20,24},{24,28},{28,32},{32,36}... | collective-permute-start | bytes 55304 | tf_op jit(solution)/shard_map/ppermute | solution.py:427
  32.8 25.5 %collective-permute-start.1 = (f32[8,12,48]{1,0,2:T(8,128)S(1)}, f32[8,12,48]{1,0,2:T(8,128)S(1)}, u32[]{:S(2)}, u32[]{:S(2)}) collective-permute-start(f32[8,12,48]{1,0,2:T(8,128)S(1)} %bitcast.53), channel_id=1, source_target_pairs={{4,0},{8,4},{12,8},{16,12},{20,16},{24,20},{28,24},{32,28},{36,32}... | collective-permute-start | bytes 55304 | tf_op jit(solution)/shard_map/ppermute | solution.py:428
  58.3 6.3 %copy-start.5 = (f32[8,24,512]{2,1,0:T(8,128)S(1)}, f32[8,24,512]{2,1,0:T(8,128)}, u32[]{:S(2)}) copy-start(f32[8,24,512]{2,1,0:T(8,128)} %constant.25.clone) | copy-start | bytes 1179652
  59.5 5.0 %collective-permute-start.2 = (f32[8,12,120]{2,1,0:T(8,128)S(1)}, f32[8,12,120]{2,1,0:T(8,128)S(1)}, u32[]{:S(2)}, u32[]{:S(2)}) collective-permute-start(f32[8,12,120]{2,1,0:T(8,128)S(1)} %get-tuple-element.44), channel_id=1, source_target_pairs={{0,64},{64,128},{128,192},{192,256},{256,320},{320,384},{384,448},... | collective-permute-start | bytes 138248 | tf_op jit(solution)/shard_map/ppermute | solution.py:427
  59.5 5.0 %collective-permute-start.3 = (f32[8,12,120]{2,1,0:T(8,128)S(1)}, f32[8,12,120]{2,1,0:T(8,128)S(1)}, u32[]{:S(2)}, u32[]{:S(2)}) collective-permute-start(f32[8,12,120]{2,1,0:T(8,128)S(1)} %get-tuple-element.45), channel_id=1, source_target_pairs={{64,0},{128,64},{192,128},{256,192},{320,256},{384,320},{448,384},... | collective-permute-start | bytes 138248 | tf_op jit(solution)/shard_map/ppermute | solution.py:428
  82.0 1.4 copy-start
  83.4 1.3 copy-start.2
  85.9 8.2 %collective-permute-start.4 = (f32[3,12,48]{2,1,0:T(8,128)S(1)}, f32[3,12,48]{2,1,0:T(8,128)S(1)}, u32[]{:S(2)}, u32[]{:S(2)}) collective-permute-start(f32[3,12,48]{2,1,0:T(8,128)S(1)} %reshape.115), channel_id=1, source_target_pairs={{0,4},{4,8},{8,12},{12,16},{16,20},{20,24},{24,28},{28,32},{32,36}... | collective-permute-start | bytes 20744 | tf_op jit(solution)/shard_map/ppermute | solution.py:427
  87.9 11.7 %collective-permute-start.5 = (f32[3,12,48]{2,1,0:T(8,128)S(1)}, f32[3,12,48]{2,1,0:T(8,128)S(1)}, u32[]{:S(2)}, u32[]{:S(2)}) collective-permute-start(f32[3,12,48]{2,1,0:T(8,128)S(1)} %reshape.117), channel_id=1, source_target_pairs={{4,0},{8,4},{12,8},{16,12},{20,16},{24,20},{28,24},{32,28},{36,32}... | collective-permute-start | bytes 20744 | tf_op jit(solution)/shard_map/ppermute | solution.py:428
  100.1 4.5 %collective-permute-start.6 = (f32[3,12,120]{2,1,0:T(8,128)S(1)}, f32[3,12,120]{2,1,0:T(8,128)S(1)}, u32[]{:S(2)}, u32[]{:S(2)}) collective-permute-start(f32[3,12,120]{2,1,0:T(8,128)S(1)} %get-tuple-element.48), channel_id=1, source_target_pairs={{0,64},{64,128},{128,192},{192,256},{256,320},{320,384},{384,448},... | collective-permute-start | bytes 51848 | tf_op jit(solution)/shard_map/ppermute | solution.py:427
  100.1 4.5 %collective-permute-start.7 = (f32[3,12,120]{2,1,0:T(8,128)S(1)}, f32[3,12,120]{2,1,0:T(8,128)S(1)}, u32[]{:S(2)}, u32[]{:S(2)}) collective-permute-start(f32[3,12,120]{2,1,0:T(8,128)S(1)} %get-tuple-element.49), channel_id=1, source_target_pairs={{64,0},{128,64},{192,128},{256,192},{320,256},{384,320},{448,384},... | collective-permute-start | bytes 51848 | tf_op jit(solution)/shard_map/ppermute | solution.py:428
  105.4 1.6 copy-start.1
  107.0 1.6 copy-start.3
  108.6 7.2 %copy-start.4 = (f32[17,24,512]{2,1,0:T(8,128)S(1)}, f32[17,24,512]{2,1,0:T(8,128)}, u32[]{:S(2)}) copy-start(f32[17,24,512]{2,1,0:T(8,128)} %get-tuple-element.38) | copy-start | bytes 2506756
  117.4 15.0 %all-to-all-start.1 = ((f32[16,1,128]{2,1,0:T(1,128)}), f32[16,1,128]{2,1,0:T(1,128)S(1)}, u32[]{:S(2)}, u32[]{:S(2)}) async-start(f32[16,1,128]{2,1,0:T(1,128)} %broadcast_in_dim.10), calls=%async_computation.1 | async-start | bytes 16384 | tf_op jit(solution)/shard_map/all_to_all | solution.py:483
  133.0 26.4 %all-to-all-start.2 = ((f32[16,1,128]{2,1,0:T(1,128)}), f32[16,1,128]{2,1,0:T(1,128)S(1)}, u32[]{:S(2)}, u32[]{:S(2)}) async-start(f32[16,1,128]{2,1,0:T(1,128)} %broadcast_in_dim.22), calls=%async_computation.2 | async-start | bytes 16384 | tf_op jit(solution)/shard_map/all_to_all | solution.py:483

commit v2 on v1

v2 whole, which is shorter than its diff:
```python
import numpy as np

import jax
import jax.numpy as jnp
from jax import lax
from jax.experimental import pallas as pl
from jax.experimental.pallas import tpu as pltpu
from jax.sharding import PartitionSpec as P

LX = 8
LY = 8
DEPTH = 3
CUTOFF = 3
LAYERS = 4
FULL_Z = DEPTH * LAYERS
HALO = 2 * CUTOFF
WIDE = LX + 2 * HALO
ATOMS = LX * LY * DEPTH
ROWS = 24
LANES = 512
HALF = FULL_Z // 2
LEVELS = HALF + 2 * CUTOFF
JITTER = 0.4
SPAN_X = LX + 2 * CUTOFF
SPAN_Y = LY + 2 * CUTOFF
SPAN_Z = DEPTH + 2 * CUTOFF
FIELDS = 17

thole_factor = 0.39
group_scale = 0.5


def within(dx, dy, dz):
    least = sum(max(abs(o) - JITTER, 0.0) ** 2 for o in (dx, dy, dz))
    return least < CUTOFF * CUTOFF


def half_offsets():
    reach = range(-CUTOFF, CUTOFF + 1)
    columns = []
    count = 0
    for dx in range(0, CUTOFF + 1):
        for dy in reach:
            depths = [
                dz
                for dz in reach
                if (dx > 0 or dy > 0 or (dy == 0 and dz > 0)) and within(dx, dy, dz)
            ]
            if depths:
                columns.append((dx, dy, depths, count))
                count += len(depths)
    return columns, count


COLUMNS, OFFSETS = half_offsets()


def may_share_group(dx, dy, dz):
    return dx == 0 and abs(DEPTH * dy + dz) <= 7 and abs(dz) < DEPTH


def lane_iota(rows=8):
    return lax.broadcasted_iota(jnp.int32, (rows, 128), 1)


def wrap_levels(value_of, out, slot, lift=0.0):
    for level in range(HALF):
        value = value_of(level)
        out[slot, CUTOFF + level] = value
        if level < CUTOFF:
            out[slot, CUTOFF + HALF + level] = pltpu.roll(value, 4, 0) + lift * HALF
        if level >= HALF - CUTOFF:
            out[slot, CUTOFF - HALF + level] = pltpu.roll(value, 4, 0) - lift * HALF


def shifted(source, field, shift, out, slot):
    if shift == 0:
        for level in range(LEVELS):
            out[slot, level] = source[field, level]
        return
    keep = lane_iota() >= shift
    for level in range(LEVELS):
        here = source[field, level]
        both = jnp.where(keep, here, pltpu.roll(here, 7, 0))
        out[slot, level] = pltpu.roll(both, 128 - shift, 1)


def spread(values, depths, shift, total):
    keep = lane_iota() >= shift
    for c in range(3):
        for level in range(-CUTOFF, HALF + CUTOFF):
            shares = [
                values[n, c, level - dz] for n, dz in enumerate(depths) if 0 <= level - dz < HALF
            ]
            if not shares:
                continue
            while len(shares) > 1:
                shares = [sum(shares[i : i + 2]) for i in range(0, len(shares), 2)]
            part = shares[0]
            if shift:
                turned = pltpu.roll(part, shift, 1)
                part = jnp.where(keep, turned, pltpu.roll(turned, 1, 0))
            total[c, CUTOFF + level] += part


def finish(polar_of, own_sum, partner_sum, out):
    for c in range(3):

        def value_of(level):
            other = CUTOFF + level + (HALF if level < CUTOFF else -HALF)
            folded = own_sum[c, level] + partner_sum[c, CUTOFF + level]
            return (folded + pltpu.roll(partner_sum[c, other], 4, 0)) * polar_of(level)

        wrap_levels(value_of, out, c)


def own_places():
    block = lax.broadcasted_iota(jnp.int32, (8, 128), 0)
    place = lane_iota() + 128 * jnp.where(block >= 4, block - 4, block)
    x = place // WIDE
    y = place - x * WIDE
    return (x >= HALO) & (x < HALO + LX) & (y >= HALO) & (y < HALO + LY)


def inner(first, second, inverse_of):
    total = jnp.zeros((8, 128), jnp.float32)
    for level in range(HALF):
        at = CUTOFF + level
        total = total + sum(first[c, at] * second[c, at] for c in range(3)) * inverse_of(level)
    return jnp.sum(jnp.where(own_places(), total, 0.0))


def apply_pass(vec, spots, spots_far, c3_ref, c5_ref, far, own_sum, partner, partner_sum):
    own_sum[...] = jnp.zeros_like(own_sum)
    partner_sum[...] = jnp.zeros_like(partner_sum)
    for number, (dx, dy, depths, first) in enumerate(COLUMNS):
        shift = dx * WIDE + dy
        for c in range(3):
            shifted(vec, c, shift, far, c)

        def per_level(level, carry):
            own = [spots[c, CUTOFF + level] for c in range(3)]
            own_u = [vec[c, CUTOFF + level] for c in range(3)]
            acc = [own_sum[c, level] for c in range(3)]
            for n, dz in enumerate(depths):
                at = CUTOFF + dz + level
                d = [spots_far[number, c, at] - own[c] for c in range(3)]
                far_u = [far[c, at] for c in range(3)]
                c3 = c3_ref[first + n, level]
                c5 = c5_ref[first + n, level]
                along_far = c5 * (d[0] * far_u[0] + d[1] * far_u[1] + d[2] * far_u[2])
                along_own = c5 * (d[0] * own_u[0] + d[1] * own_u[1] + d[2] * own_u[2])
                for c in range(3):
                    acc[c] = acc[c] + (along_far * d[c] - c3 * far_u[c])
                    partner[n, c, level] = along_own * d[c] - c3 * own_u[c]
            for c in range(3):
                own_sum[c, level] = acc[c]
            return carry

        lax.fori_loop(0, HALF, per_level, 0, unroll=2)
        spread(partner, depths, shift, partner_sum)


def pack_kernel(spot_ref, polar_ref, direct_ref, group_ref, out_ref, rows):
    site = lax.broadcasted_iota(jnp.int32, (1, ATOMS), 1)
    x = site // (LY * DEPTH)
    y = site // DEPTH - LY * x
    z = site - DEPTH * (site // DEPTH)
    for c, lattice in enumerate((x, y, z)):
        rows[c : c + 1] = spot_ref[c, 0, 0] - lattice.astype(jnp.float32)
        rows[4 + c : 5 + c] = polar_ref[0, 0] * direct_ref[c, 0, 0]
    rows[3:4] = polar_ref[0, 0]
    rows[7:8] = group_ref[0, 0].astype(jnp.float32)
    old = lax.broadcasted_iota(jnp.int32, (ATOMS, ATOMS), 0)
    new = lax.broadcasted_iota(jnp.int32, (ATOMS, ATOMS), 1)
    plane = new // (LX * LY)
    order = jnp.where(old == DEPTH * (new - LX * LY * plane) + plane, 1.0, 0.0)
    packed = jnp.dot(
        rows[...], order, precision=lax.Precision.HIGHEST, preferred_element_type=jnp.float32
    )
    for n in range(LAYERS):
        out_ref[n] = packed


def first_kernel(
    base_ref, c3_ref, c5_ref, u1_ref, u2_ref, moment_ref,
    fields, far, own_sum, partner, partner_sum, vec, vec_b, spots_far,
):
    for f in range(3):
        wrap_levels(lambda level: base_ref[f, level], fields, f, 1.0 if f == 2 else 0.0)
        wrap_levels(lambda level: base_ref[4 + f, level], vec, f)
    wrap_levels(lambda level: (thole_factor**0.5) * lax.rsqrt(base_ref[3, level]), fields, 3)
    wrap_levels(lambda level: base_ref[7, level], fields, 4)
    polar_of = lambda level: base_ref[3, level]
    inverse_of = lambda level: 1.0 / base_ref[3, level]

    own_sum[...] = jnp.zeros_like(own_sum)
    partner_sum[...] = jnp.zeros_like(partner_sum)
    for number, (dx, dy, depths, first) in enumerate(COLUMNS):
        shift = dx * WIDE + dy
        for c in range(3):
            shifted(fields, c, shift, spots_far.at[number], c)
            shifted(vec, c, shift, far, c)
        shifted(fields, 3, shift, far, 3)
        if dx == 0:
            shifted(fields, 4, shift, far, 4)

        def per_level(level, carry):
            own = [fields[c, CUTOFF + level] for c in range(3)]
            root = fields[3, CUTOFF + level]
            own_u = [vec[c, CUTOFF + level] for c in range(3)]
            acc = [own_sum[c, level] for c in range(3)]
            for n, dz in enumerate(depths):
                at = CUTOFF + dz + level
                d = [spots_far[number, c, at] - own[c] for c in range(3)]
                far_u = [far[c, at] for c in range(3)]
                s = d[0] * d[0] + d[1] * d[1] + d[2] * d[2]
                inv = lax.rsqrt(s)
                inv2 = inv * inv
                inv3 = inv2 * inv
                x = (s * s * inv) * (root * far[3, at])
                e = jnp.exp(-x)
                l3 = 1.0 - e
                l5 = l3 - x * e
                cut = jnp.maximum(1.0 - s * (1.0 / (CUTOFF * CUTOFF)), 0.0)
                weight = cut * cut * inv3
                if may_share_group(dx, dy, dz):
                    same = fields[4, CUTOFF + level] == far[4, at]
                    weight = jnp.where(same, group_scale * weight, weight)
                c3 = weight * l3
                c5 = (3.0 * weight) * (inv2 * l5)
                c3_ref[first + n, level] = c3
                c5_ref[first + n, level] = c5
                along_far = c5 * (d[0] * far_u[0] + d[1] * far_u[1] + d[2] * far_u[2])
                along_own = c5 * (d[0] * own_u[0] + d[1] * own_u[1] + d[2] * own_u[2])
                for c in range(3):
                    acc[c] = acc[c] + (along_far * d[c] - c3 * far_u[c])
                    partner[n, c, level] = along_own * d[c] - c3 * own_u[c]
            for c in range(3):
                own_sum[c, level] = acc[c]
            return carry

        lax.fori_loop(0, HALF, per_level, 0, unroll=2)
        spread(partner, depths, shift, partner_sum)
    finish(polar_of, own_sum, partner_sum, vec_b)
    moments = [inner(vec, vec, inverse_of), inner(vec, vec_b, inverse_of), inner(vec_b, vec_b, inverse_of)]
    for c in range(3):
        for level in range(HALF):
            u1_ref[c, level] = vec_b[c, CUTOFF + level]
    apply_pass(vec_b, fields, spots_far, c3_ref, c5_ref, far, own_sum, partner, partner_sum)
    finish(polar_of, own_sum, partner_sum, vec)
    moments += [inner(vec_b, vec, inverse_of), inner(vec, vec, inverse_of)]
    for c in range(3):
        for level in range(HALF):
            u2_ref[c, level] = vec[c, CUTOFF + level]
    lane = lax.broadcasted_iota(jnp.int32, (1, 128), 1)
    row = jnp.zeros((1, 128), jnp.float32)
    for n, value in enumerate(moments):
        row = jnp.where(lane == n, value, row)
    moment_ref[...] = row


def lay_planes(layer, base_ref, u1_ref, u2_ref, u3, stage, far_ref):
    lane = lane_iota(ROWS)
    row = lax.broadcasted_iota(jnp.int32, (ROWS, 128), 0)
    for z in range(-CUTOFF, FULL_Z + CUTOFF):
        half, level = z % FULL_Z // HALF, z % HALF
        values = [base_ref[f, level] for f in (0, 1, 2, 3, 7, 4, 5, 6)]
        values[2] = values[2] + float(z - level)
        values[3] = (thole_factor**0.5) * lax.rsqrt(values[3])
        values += [u1_ref[c, level] for c in range(3)]
        values += [u2_ref[c, level] for c in range(3)]
        values += [u3[c, CUTOFF + level] for c in range(3)]
        for n, value in enumerate(values):
            stage[CUTOFF + z, 4 * n : 4 * n + 4] = value[4 * half : 4 * half + 4]

    def staged(z, b):
        return stage[layer * DEPTH + z, pl.ds(b, ROWS, stride=4), :]

    for x in range(SPAN_X):
        begin = (x + HALO - CUTOFF) * WIDE + HALO - CUTOFF
        b, offset = begin // 128, begin % 128
        plane = jnp.where(row < 3, 1.0e3, 0.0)
        for z in range(SPAN_Z):
            goal = z * SPAN_Y
            shift = (goal - offset) % 128
            piece = pltpu.roll(staged(z, b), shift, 1) if shift else staged(z, b)
            if offset + SPAN_Y > 128:
                more = pltpu.roll(staged(z, b + 1), shift, 1) if shift else staged(z, b + 1)
                piece = jnp.where(lane < goal + 128 - offset, piece, more)
            plane = jnp.where((lane >= goal) & (lane < goal + SPAN_Y), piece, plane)
        far_ref[x] = jnp.where(row < FIELDS, plane, 0.0)


def second_kernel(
    layer_ref, base_ref, c3_ref, c5_ref, u1_ref, u2_ref, moment_in, far_ref, moment_ref,
    fields, far, own_sum, partner, partner_sum, vec, vec_b, spots_far, stage,
):
    for f in range(3):
        wrap_levels(lambda level: base_ref[f, level], fields, f, 1.0 if f == 2 else 0.0)
        wrap_levels(lambda level: u2_ref[f, level], vec, f)
    polar_of = lambda level: base_ref[3, level]
    inverse_of = lambda level: 1.0 / base_ref[3, level]
    for number, (dx, dy, _, _) in enumerate(COLUMNS):
        for c in range(3):
            shifted(fields, c, dx * WIDE + dy, spots_far.at[number], c)
    apply_pass(vec, fields, spots_far, c3_ref, c5_ref, far, own_sum, partner, partner_sum)
    finish(polar_of, own_sum, partner_sum, vec_b)
    lay_planes(layer_ref[0], base_ref, u1_ref, u2_ref, vec_b, stage, far_ref)
    lane = lax.broadcasted_iota(jnp.int32, (1, 128), 1)
    moment_ref[...] = jnp.where(lane == 5, inner(vec, vec_b, inverse_of), moment_in[...])


def gradient_kernel(moment_ref, far_ref, dipole_ref, force_ref, energy_ref, turned, out_ref):
    total = jnp.sum(moment_ref[...], axis=0, keepdims=True)
    lane = lax.broadcasted_iota(jnp.int32, (1, 128), 1)

    def pick(n):
        return jnp.sum(jnp.where(lane == n, total, 0.0), axis=1, keepdims=True)

    m0, m1, m2, m3, m4, m5 = (pick(n) for n in range(6))
    g = m2 / (m2 - m3)
    rest = 1.0 - g
    rz1 = rest * rest * m2 + 2.0 * g * rest * m3 + g * g * m4
    a = rest + rz1 / m2
    curve = a * a * (m2 - m3) + 2.0 * a * g * (m3 - m4) + g * g * (m4 - m5)
    g1 = rz1 / curve
    k1 = g + g1 * a
    k2 = g1 * g
    energy_ref[...] = -(m0 + k1 * m1 + k2 * m2)
    far_k1 = jnp.broadcast_to(k1, (1, 128))
    far_k2 = jnp.broadcast_to(k2, (1, 128))

    def plane(x, carry):
        far = []
        for n in range(2 * CUTOFF + 1):
            block = far_ref[x + n]
            spot = [block[c : c + 1] for c in range(5)]
            u = [[block[5 + 3 * q + c : 6 + 3 * q + c] for c in range(3)] for q in range(4)]
            dip = [u[0][c] + far_k1 * u[1][c] + far_k2 * u[2][c] for c in range(3)]
            adj = [u[0][c] + u[1][c] + far_k1 * u[2][c] + far_k2 * u[3][c] for c in range(3)]
            far.append((spot, dip, adj))
        turned[...] = jnp.transpose(far_ref[x + CUTOFF])
        for t in range(DEPTH):
            start = pl.multiple_of(x * (LY * DEPTH) + 8 * t, 8)
            own_block = turned[pl.ds((t + CUTOFF) * SPAN_Y + CUTOFF, LY), :]

            def own_field(n):
                return jnp.broadcast_to(own_block[:, n : n + 1], (8, 128))

            spot_i = [own_field(c) for c in range(5)]
            u = [[own_field(5 + 3 * q + c) for c in range(3)] for q in range(4)]
            dip_i = [u[0][c] + k1 * u[1][c] + k2 * u[2][c] for c in range(3)]
            adj_i = [u[0][c] + u[1][c] + k1 * u[2][c] + k2 * u[3][c] for c in range(3)]
            acc = [jnp.zeros((8, 128), jnp.float32) for _ in range(3)]
            for n in range(2 * CUTOFF + 1):
                spot, dip, adj = far[n]
                d = [spot[c] - spot_i[c] for c in range(3)]
                s = d[0] * d[0] + d[1] * d[1] + d[2] * d[2]
                if n == CUTOFF:
                    own_atom = s == 0.0
                    s = jnp.where(own_atom, 1.0, s)
                inv = lax.rsqrt(s)
                inv2 = inv * inv
                x_damp = (s * s * inv) * (spot_i[3] * spot[3])
                xe = x_damp * jnp.exp(-x_damp)
                e = jnp.exp(-x_damp)
                l3 = 1.0 - e
                l5 = l3 - xe
                cut = jnp.maximum(1.0 - s * (1.0 / (CUTOFF * CUTOFF)), 0.0)
                scale = inv2 * inv
                if n == CUTOFF:
                    scale = jnp.where(spot[4] == spot_i[4], group_scale * scale, scale)
                    scale = jnp.where(own_atom, 0.0, scale)
                ratio = cut * inv2
                scale = scale * cut
                scale5 = 3.0 * scale * inv2
                c5 = scale5 * cut * l5
                slope3 = scale * ((-4.0 / (CUTOFF * CUTOFF)) * l3 - 3.0 * ratio * l5)
                slope5 = scale5 * (
                    (-4.0 / (CUTOFF * CUTOFF)) * l5 + ratio * (3.0 * x_damp * xe - 5.0 * l5)
                )
                own_dip = d[0] * dip_i[0] + d[1] * dip_i[1] + d[2] * dip_i[2]
                own_adj = d[0] * adj_i[0] + d[1] * adj_i[1] + d[2] * adj_i[2]
                far_dip = d[0] * dip[0] + d[1] * dip[1] + d[2] * dip[2]
                far_adj = d[0] * adj[0] + d[1] * adj[1] + d[2] * adj[2]
                cross = (
                    dip_i[0] * adj[0] + dip_i[1] * adj[1] + dip_i[2] * adj[2]
                    + adj_i[0] * dip[0] + adj_i[1] * dip[1] + adj_i[2] * dip[2]
                )
                radial = slope5 * (own_dip * far_adj + own_adj * far_dip) - slope3 * cross
                p1, p2, p3, p4 = c5 * own_dip, c5 * far_adj, c5 * own_adj, c5 * far_dip
                for c in range(3):
                    acc[c] = acc[c] + (
                        radial * d[c] + p1 * adj[c] + p2 * dip_i[c] + p3 * dip[c] + p4 * adj_i[c]
                    )
            lanes = lax.broadcasted_iota(jnp.int32, (8, 128), 1)
            result = jnp.zeros((8, 128), jnp.float32)
            for c in range(3):
                result = jnp.where(lanes == c, dip_i[c], result)
                force = -0.5 * jnp.sum(acc[c], axis=1, keepdims=True)
                result = jnp.where(lanes == 3 + c, force, result)
            out_ref[pl.ds(start, 8), :] = result
        return carry

    lax.fori_loop(0, LX, plane, 0)
    old = lax.broadcasted_iota(jnp.int32, (ATOMS, ATOMS), 0)
    new = lax.broadcasted_iota(jnp.int32, (ATOMS, ATOMS), 1)
    x = new // (LY * DEPTH)
    y = new // DEPTH - LY * x
    z = new - DEPTH * (new // DEPTH)
    order = jnp.where(old == (x * DEPTH + z) * LY + y, 1.0, 0.0)
    result = jnp.dot(
        jnp.transpose(out_ref[...])[:8],
        order,
        precision=lax.Precision.HIGHEST,
        preferred_element_type=jnp.float32,
    )
    for c in range(3):
        dipole_ref[c, 0, 0] = result[c : c + 1]
        force_ref[c, 0, 0] = result[3 + c : 4 + c]


def vmem_specs(count):
    return [pl.BlockSpec(memory_space=pltpu.VMEM)] * count


F32 = jnp.float32
SCRATCH = [
    pltpu.VMEM((5, LEVELS, 8, 128), F32),
    pltpu.VMEM((5, LEVELS, 8, 128), F32),
    pltpu.VMEM((3, HALF, 8, 128), F32),
    pltpu.VMEM((2 * CUTOFF + 1, 3, HALF, 8, 128), F32),
    pltpu.VMEM((3, LEVELS, 8, 128), F32),
    pltpu.VMEM((3, LEVELS, 8, 128), F32),
    pltpu.VMEM((3, LEVELS, 8, 128), F32),
    pltpu.VMEM((len(COLUMNS), 3, LEVELS, 8, 128), F32),
]
COUPLING = jax.ShapeDtypeStruct((OFFSETS, HALF, 8, 128), F32)
VECTOR = jax.ShapeDtypeStruct((3, HALF, 8, 128), F32)
PARAMS = pltpu.CompilerParams(vmem_limit_bytes=16 * 1024 * 1024)


def run_pack(positions, polarizability, direct_field, groups):
    return pl.pallas_call(
        pack_kernel,
        out_shape=jax.ShapeDtypeStruct((LAYERS, 8, ATOMS), F32),
        in_specs=vmem_specs(4),
        out_specs=vmem_specs(1)[0],
        scratch_shapes=[pltpu.VMEM((8, ATOMS), F32)],
        compiler_params=PARAMS,
    )(positions, polarizability, direct_field, groups)


def run_first(base):
    outs = (
        COUPLING,
        COUPLING,
        VECTOR,
        VECTOR,
        jax.ShapeDtypeStruct((1, 128), F32),
    )
    return pl.pallas_call(
        first_kernel,
        out_shape=outs,
        in_specs=vmem_specs(1),
        out_specs=tuple(vmem_specs(len(outs))),
        scratch_shapes=SCRATCH,
        compiler_params=PARAMS,
    )(base)


def run_second(layer, base, c3, c5, u1, u2, moments):
    outs = (
        jax.ShapeDtypeStruct((SPAN_X, ROWS, 128), F32),
        jax.ShapeDtypeStruct((1, 128), F32),
    )
    return pl.pallas_call(
        second_kernel,
        out_shape=outs,
        in_specs=[pl.BlockSpec(memory_space=pltpu.SMEM)] + vmem_specs(6),
        out_specs=tuple(vmem_specs(2)),
        scratch_shapes=SCRATCH + [pltpu.VMEM((FULL_Z + 2 * CUTOFF, 4 * ROWS, 128), F32)],
        compiler_params=PARAMS,
    )(layer, base, c3, c5, u1, u2, moments)


def run_gradient(moments, far):
    return pl.pallas_call(
        gradient_kernel,
        out_shape=(
            jax.ShapeDtypeStruct((3, 1, 1, 1, ATOMS), F32),
            jax.ShapeDtypeStruct((3, 1, 1, 1, ATOMS), F32),
            jax.ShapeDtypeStruct((1, 1), F32),
        ),
        in_specs=vmem_specs(2),
        out_specs=tuple(vmem_specs(3)),
        scratch_shapes=[pltpu.VMEM((128, ROWS), F32), pltpu.VMEM((ATOMS, 128), F32)],
        compiler_params=PARAMS,
    )(moments, far)


def both_sides(low, high, axis):
    count = lax.axis_size(axis)
    below = lax.ppermute(high, axis, [(i, (i + 1) % count) for i in range(count)])
    above = lax.ppermute(low, axis, [((i + 1) % count, i) for i in range(count)])
    return below, above


def widen_x(along_y):
    below, above = both_sides(
        along_y[..., : HALO * WIDE], along_y[..., (LX - HALO) * WIDE :], "gx"
    )
    flat = jnp.concatenate([below, along_y, above], axis=-1)
    flat = jnp.pad(flat, ((0, 0), (0, 0), (0, LANES - WIDE * WIDE)))
    halves = flat.reshape(flat.shape[0], 2, HALF, LANES // 128, 128)
    return halves.transpose(0, 2, 1, 3, 4).reshape(flat.shape[0], HALF, 8, 128)


def join_y(below, own, above):
    lead = own.shape[0]
    return jnp.concatenate([below, own, above], axis=-1).reshape(lead, FULL_Z, LX * WIDE)


def frame_constants():
    place = np.arange(LANES)
    x, y = place // WIDE, place % WIDE
    z = np.arange(FULL_Z)
    full = np.zeros((8, FULL_Z, LANES), np.float32)
    full[0] = (x - HALO)[None, :]
    full[1] = (y - HALO)[None, :]
    full[2] = (z % HALF)[:, None]
    full[3] = np.where(place >= WIDE * WIDE, 0.05, 0.0)[None, :]
    domain = (x + 2) // LX * 8 + (y + 2) // LY
    full[7] = 64.0 * (domain[None, :] * LAYERS + (z // DEPTH)[:, None])
    halves = full.reshape(8, 2, HALF, LANES // 128, 128).transpose(0, 2, 1, 3, 4)
    return halves.reshape(8, HALF, 8, 128)


def on_device(positions, polarizability, direct_field, groups):
    layer = lax.axis_index("gz")
    copies = run_pack(positions, polarizability, direct_field, groups)
    column = lax.all_to_all(copies, "gz", 0, 0)
    below, above = both_sides(column, column, "gy")
    lattices = [
        part.reshape(LAYERS, 8, DEPTH, LX, LY).transpose(1, 0, 2, 3, 4).reshape(8, FULL_Z, LX, LY)
        for part in (below, column, above)
    ]
    along_y = join_y(lattices[0][..., LY - HALO :], lattices[1], lattices[2][..., :HALO])
    base = widen_x(along_y) + frame_constants()
    c3, c5, u1, u2, moments = run_first(base)
    flat_u2 = u2.reshape(3, HALF, 2, LANES).transpose(0, 2, 1, 3).reshape(3, FULL_Z, LANES)
    own_u2 = flat_u2[..., HALO * WIDE : (HALO + LX) * WIDE].reshape(3, FULL_Z, LX, WIDE)
    own_u2 = own_u2[..., HALO : HALO + LY]
    low = own_u2[..., :HALO].reshape(3, FULL_Z, LX * HALO)
    high = own_u2[..., LY - HALO :].reshape(3, FULL_Z, LX * HALO)
    below, above = both_sides(low, high, "gy")
    cut = (3, FULL_Z, LX, HALO)
    u2_wide = widen_x(join_y(below.reshape(cut), own_u2, above.reshape(cut)))
    far, moments = run_second(layer[None], base, c3, c5, u1, u2_wide, moments)
    moments, far = lax.optimization_barrier((moments, far))
    for axis in ("gx", "gy"):
        count = lax.axis_size(axis)
        copies = jnp.broadcast_to(moments[None], (count, 1, 128))
        moments = lax.all_to_all(copies, axis, 0, 0).reshape(count, 128)
        if axis == "gx":
            moments = jnp.sum(moments, axis=0, keepdims=True)
    dipoles, gradient, energy = run_gradient(moments, far)
    devices = lax.axis_size("gx") * lax.axis_size("gy") * lax.axis_size("gz")
    return (dipoles, gradient, (energy / (2.0 * ATOMS * devices)).reshape(()))


def solution(mesh):
    along = ("gx", "gy", "gz", None)
    return jax.shard_map(
        on_device,
        mesh=mesh,
        in_specs=(P(None, *along), P(*along), P(None, *along), P(*along)),
        out_specs=(P(None, *along), P(None, *along), P()),
        check_vma=False,
    )
```

time: 168 us -> 140 us (0.83)
  blocking collectives: 12.7 us -> 54.2 us
  waiting for transfers between devices: 49.2 us -> 21.7 us
  starting transfers between devices: 45.8 us -> 24.7 us
  local copies, waits for them, and re-layouts: 21.4 us -> 7.9 us
  other arithmetic: 6.39 us -> 0.66 us
  Pallas kernels: 28.5 us -> 26.7 us
    all_to_all x1 -> x3, blocking collectives: 12.7 us -> 54.2 us  [the longest x2 41.5 us: on_device(): moments = lax.all_to_all(copies, axis, 0, 0).reshape(count, 128)]
    all_to_all x2 -> x0, starting transfers between devices: 21 us -> none  [on_device(): moments = lax.all_to_all(copies, axis, 0, 0).reshape(count, 128)]
    all_to_all x2 -> x0, waiting for transfers between devices: 18 us -> none  [on_device(): moments = lax.all_to_all(copies, axis, 0, 0).reshape(count, 128)]
    ppermute x4, waiting for transfers between devices: 10.3 us -> 3.28 us  [both_sides(): lax.ppermute(high, axis, [(i, (i + 1) % count) for i in range(count)])]
    unnamed x22 -> x14, local copies, waits for them, and re-layouts: 10.6 us -> 5.69 us
    unnamed x4 -> x0, other arithmetic: 3.39 us -> none
    pallas_call x1, Pallas kernels: 17.3 us -> 14.3 us  [run_first(): pl.pallas_call(first_kernel, out_shape=outs, in_specs=vmem_specs(1), out_...]
    ppermute x4, waiting for transfers between devices: 20.9 us -> 18.4 us  [both_sides(): lax.ppermute(low, axis, [((i + 1) % count, i) for i in range(count)])]
  transfers between devices with their start and end apart: 10 -> 8, of which waited for: 7 -> 4; matrix products, arithmetic and copies ran while one was open for 4% -> 1% of each run, Pallas kernels for 0% -> 0%
where the time goes in v2:
time: 140 us; the launch traced here: 139 us
  blocking collectives  54.2 us (39%)
  Pallas kernels  26.7 us (19%)
  starting transfers between devices  24.7 us (18%)
  waiting for transfers between devices  21.7 us (16%)
  local copies, waits for them, and re-layouts  7.9 us (6%)
  between operations  2.73 us (2%)
    all_to_all x2, blocking collectives, on_device(): moments = lax.all_to_all(copies, axis, 0, 0).reshape(count, 128)  41.5 us
    ppermute x4, waiting for transfers between devices, both_sides(): lax.ppermute(low, axis, [((i + 1) % count, i) for i in range(count)])  18.4 us
    pallas_call x1, Pallas kernels, run_first(): pl.pallas_call(first_kernel, out_shape=outs, in_specs=vmem_specs(1), out_...  14.3 us
    ppermute x4, starting transfers between devices, both_sides(): lax.ppermute(high, axis, [(i, (i + 1) % count) for i in range(count)])  12.8 us
    all_to_all x1, blocking collectives, on_device(): column = lax.all_to_all(copies, 'gz', 0, 0)  12.7 us
    ppermute x4, starting transfers between devices, both_sides(): lax.ppermute(low, axis, [((i + 1) % count, i) for i in range(count)])  11.9 us
    pallas_call x1, Pallas kernels, run_second(): pl.pallas_call(second_kernel, out_shape=outs, in_specs=[pl.BlockSpec(memo...  6.71 us
    unnamed x14, local copies, waits for them, and re-layouts  5.69 us
  transfers between devices with their start and end apart: 8, of which 4 were waited for; matrix products, arithmetic and copies ran while one was open for 1% of the time, Pallas kernels for 0%

profile of v2, /device:TPU:6, one launch (start us, length us, event | category | flops | bytes accessed | tf_op | source)
XLA Modules:
  0.0 138.6 jit_solution(1860387148715192276)
XLA Ops:
  0.6 0.7 copy-done.2
  1.3 0.7 copy-done.3
  2.0 0.7 copy-done.4
  2.7 0.7 copy-done.5
  3.4 0.2 shard_map.76
  3.6 12.7 %all_to_all.15 = f32[4,8,192]{2,1,0:T(8,128)S(1)} all-to-all(f32[4,8,192]{2,1,0:T(8,128)S(1)} %shard_map.76), channel_id=1, replica_groups=mesh['gx'=16,'gy'=16,'gz'=4] {'gz'}, dimensions={0} | all-to-all | bytes 49152 | tf_op jit(solution)/shard_map/all_to_all | solution.py:543
  16.3 10.8 %collective-permute-start = (f32[4,8,192]{2,1,0:T(8,128)S(1)}, f32[4,8,192]{2,1,0:T(8,128)S(1)}, u32[]{:S(2)}, u32[]{:S(2)}) collective-permute-start(f32[4,8,192]{2,1,0:T(8,128)S(1)} %all_to_all.15), channel_id=1, source_target_pairs={{0,4},{4,8},{8,12},{12,16},{16,20},{20,24},{24,28},{28,32},{32,36}... | collective-permute-start | bytes 73736 | tf_op jit(solution)/shard_map/ppermute | solution.py:505
  27.1 1.9 %collective-permute-start.1 = (f32[4,8,192]{2,1,0:T(8,128)S(1)}, f32[4,8,192]{2,1,0:T(8,128)S(1)}, u32[]{:S(2)}, u32[]{:S(2)}) collective-permute-start(f32[4,8,192]{2,1,0:T(8,128)S(1)} %all_to_all.15), channel_id=1, source_target_pairs={{4,0},{8,4},{12,8},{16,12},{20,16},{24,20},{28,24},{32,28},{36,32}... | collective-permute-start | bytes 73736 | tf_op jit(solution)/shard_map/ppermute | solution.py:506
  29.7 10.3 %collective-permute-done.1 = f32[4,8,192]{2,1,0:T(8,128)S(1)} collective-permute-done((f32[4,8,192]{2,1,0:T(8,128)S(1)}, f32[4,8,192]{2,1,0:T(8,128)S(1)}, u32[]{:S(2)}, u32[]{:S(2)}) %collective-permute-start.1) | collective-permute-done | bytes 24608 | tf_op jit(solution)/shard_map/ppermute | solution.py:506
  40.2 0.3 pad_maximum_fusion
  40.8 3.0 %collective-permute-start.3 = (f32[8,12,120]{2,0,1:T(8,128)S(1)}, f32[8,12,120]{2,0,1:T(8,128)S(1)}, u32[]{:S(2)}, u32[]{:S(2)}) collective-permute-start(f32[8,12,120]{2,0,1:T(8,128)S(1)} %get-tuple-element.30), channel_id=1, source_target_pairs={{64,0},{128,64},{192,128},{256,192},{320,256},{384,320},{448,384},... | collective-permute-start | bytes 138248 | tf_op jit(solution)/shard_map/ppermute | solution.py:506
  43.8 1.8 %collective-permute-done.2 = f32[8,12,120]{2,0,1:T(8,128)S(1)} collective-permute-done((f32[8,12,120]{2,0,1:T(8,128)S(1)}, f32[8,12,120]{2,0,1:T(8,128)S(1)}, u32[]{:S(2)}, u32[]{:S(2)}) %collective-permute-start.2) | collective-permute-done | bytes 46112 | tf_op jit(solution)/shard_map/ppermute | solution.py:505
  45.7 14.3 %shard_map.77 = (f32[89,6,8,128]{3,2,1,0:T(8,128)S(1)}, f32[89,6,8,128]{3,2,1,0:T(8,128)S(1)}, f32[3,6,8,128]{3,2,1,0:T(8,128)S(1)}, f32[3,6,8,128]{3,2,1,0:T(8,128)S(1)}, f32[1,128]{1,0:T(1,128)S(1)}) custom-call(f32[8,6,8,128]{3,2,1,0:T(8,128)S(1)} %bitcast.34), custom_call_target="tpu_custom_call" | custom-call | tf_op jit(solution)/shard_map/pallas_call | solution.py:463
  60.0 1.4 copy-done
  61.9 1.9 %collective-permute-start.4 = (f32[3,12,48]{2,1,0:T(8,128)S(1)}, f32[3,12,48]{2,1,0:T(8,128)S(1)}, u32[]{:S(2)}, u32[]{:S(2)}) collective-permute-start(f32[3,12,48]{2,1,0:T(8,128)S(1)} %reshape.88), channel_id=1, source_target_pairs={{0,4},{4,8},{8,12},{12,16},{16,20},{20,24},{24,28},{28,32},{32,36}... | collective-permute-start | bytes 20744 | tf_op jit(solution)/shard_map/ppermute | solution.py:505
  63.9 4.1 %collective-permute-start.5 = (f32[3,12,48]{2,1,0:T(8,128)S(1)}, f32[3,12,48]{2,1,0:T(8,128)S(1)}, u32[]{:S(2)}, u32[]{:S(2)}) collective-permute-start(f32[3,12,48]{2,1,0:T(8,128)S(1)} %reshape.90), channel_id=1, source_target_pairs={{4,0},{8,4},{12,8},{16,12},{20,16},{24,20},{28,24},{32,28},{36,32}... | collective-permute-start | bytes 20744 | tf_op jit(solution)/shard_map/ppermute | solution.py:506
  68.3 8.0 %collective-permute-done.5 = f32[3,12,48]{2,1,0:T(8,128)S(1)} collective-permute-done((f32[3,12,48]{2,1,0:T(8,128)S(1)}, f32[3,12,48]{2,1,0:T(8,128)S(1)}, u32[]{:S(2)}, u32[]{:S(2)}) %collective-permute-start.5) | collective-permute-done | bytes 6944 | tf_op jit(solution)/shard_map/ppermute | solution.py:506
  76.8 2.9 %collective-permute-start.7 = (f32[3,12,120]{2,1,0:T(8,128)S(1)}, f32[3,12,120]{2,1,0:T(8,128)S(1)}, u32[]{:S(2)}, u32[]{:S(2)}) collective-permute-start(f32[3,12,120]{2,1,0:T(8,128)S(1)} %get-tuple-element.32), channel_id=1, source_target_pairs={{64,0},{128,64},{192,128},{256,192},{320,256},{384,320},{448,384},... | collective-permute-start | bytes 51848 | tf_op jit(solution)/shard_map/ppermute | solution.py:506
  79.7 1.5 %collective-permute-done.6 = f32[3,12,120]{2,1,0:T(8,128)S(1)} collective-permute-done((f32[3,12,120]{2,1,0:T(8,128)S(1)}, f32[3,12,120]{2,1,0:T(8,128)S(1)}, u32[]{:S(2)}, u32[]{:S(2)}) %collective-permute-start.6) | collective-permute-done | bytes 17312 | tf_op jit(solution)/shard_map/ppermute | solution.py:505
  81.4 1.6 %copy-done.1 = f32[89,6,8,128]{3,2,1,0:T(8,128)S(1)} copy-done((f32[89,6,8,128]{3,2,1,0:T(8,128)S(1)}, f32[89,6,8,128]{3,2,1,0:T(8,128)}, u32[]{:S(2)}) %copy-start.1) | copy-done | bytes 2187288
  83.0 6.7 %shard_map.78 = (f32[14,24,128]{2,1,0:T(8,128)S(1)}, f32[1,128]{1,0:T(1,128)S(1)}) custom-call(s32[1]{0:T(128)} %bitcast.layer_ref, f32[8,6,8,128]{3,2,1,0:T(8,128)S(1)} %bitcast.35, f32[89,6,8,128]{3,2,1,0:T(8,128)S(1)} %get-tuple-element.15.c3_ref, f32[89,6,8,128]{3,2,1,0:T(8,128)S(1)} %copy-done.1, f32[3,6,8,128]{3,2,1,0:T(8,128)S(1)} %get-tuple-element.17.u1_ref, ...), custom_call_target="tpu_custom_call" | custom-call | tf_op jit(solution)/shard_map/pallas_call | solution.py:478
  89.7 14.3 %all_to_all.16 = f32[16,1,128]{2,1,0:T(1,128)S(1)} all-to-all(f32[16,1,128]{2,1,0:T(1,128)S(1)} %broadcast_in_dim.18), channel_id=1, replica_groups=mesh['gx'=16,'gy'=16,'gz'=4] {'gx'}, dimensions={0} | all-to-all | bytes 16384 | tf_op jit(solution)/shard_map/all_to_all | solution.py:565
  104.1 27.1 %all_to_all.17 = f32[16,1,128]{2,1,0:T(1,128)S(1)} all-to-all(f32[16,1,128]{2,1,0:T(1,128)S(1)} %broadcast_in_dim.19), channel_id=1, replica_groups=mesh['gx'=16,'gy'=16,'gz'=4] {'gy'}, dimensions={0} | all-to-all | bytes 16384 | tf_op jit(solution)/shard_map/all_to_all | solution.py:565
  131.2 5.6 %shard_map.79 = (f32[3,1,1,1,192]{4,3,2,1,0:T(1,128)}, f32[3,1,1,1,192]{4,3,2,1,0:T(1,128)}, f32[1,1]{1,0:T(1,128)}) custom-call(f32[16,128]{1,0:T(8,128)S(1)} %bitcast.37, f32[14,24,128]{2,1,0:T(8,128)S(1)} %get-tuple-element.23.far_ref), custom_call_target="tpu_custom_call" | custom-call | tf_op jit(solution)/shard_map/pallas_call | solution.py:489
  (46 shorter events, 2.7 us)
Async XLA Ops:
  0.6 0.7 copy-start.2
  1.3 0.7 copy-start.3
  2.0 0.7 copy-start.4
  2.7 0.7 copy-start.5
  16.3 13.0 %collective-permute-start = (f32[4,8,192]{2,1,0:T(8,128)S(1)}, f32[4,8,192]{2,1,0:T(8,128)S(1)}, u32[]{:S(2)}, u32[]{:S(2)}) collective-permute-start(f32[4,8,192]{2,1,0:T(8,128)S(1)} %all_to_all.15), channel_id=1, source_target_pairs={{0,4},{4,8},{8,12},{12,16},{16,20},{20,24},{24,28},{28,32},{32,36}... | collective-permute-start | bytes 73736 | tf_op jit(solution)/shard_map/ppermute | solution.py:505
  27.1 12.9 %collective-permute-start.1 = (f32[4,8,192]{2,1,0:T(8,128)S(1)}, f32[4,8,192]{2,1,0:T(8,128)S(1)}, u32[]{:S(2)}, u32[]{:S(2)}) collective-permute-start(f32[4,8,192]{2,1,0:T(8,128)S(1)} %all_to_all.15), channel_id=1, source_target_pairs={{4,0},{8,4},{12,8},{16,12},{20,16},{24,20},{28,24},{32,28},{36,32}... | collective-permute-start | bytes 73736 | tf_op jit(solution)/shard_map/ppermute | solution.py:506
  29.5 16.1 %copy-start.6 = (f32[8,12,512]{2,0,1:T(8,128)S(1)}, f32[8,12,512]{2,0,1:T(8,128)}, u32[]{:S(2)}) copy-start(f32[8,12,512]{2,0,1:T(8,128)} %constant.24) | copy-start | bytes 589828
  40.8 4.7 %collective-permute-start.2 = (f32[8,12,120]{2,0,1:T(8,128)S(1)}, f32[8,12,120]{2,0,1:T(8,128)S(1)}, u32[]{:S(2)}, u32[]{:S(2)}) collective-permute-start(f32[8,12,120]{2,0,1:T(8,128)S(1)} %get-tuple-element.29), channel_id=1, source_target_pairs={{0,64},{64,128},{128,192},{192,256},{256,320},{320,384},{384,448},... | collective-permute-start | bytes 138248 | tf_op jit(solution)/shard_map/ppermute | solution.py:505
  40.8 4.7 %collective-permute-start.3 = (f32[8,12,120]{2,0,1:T(8,128)S(1)}, f32[8,12,120]{2,0,1:T(8,128)S(1)}, u32[]{:S(2)}, u32[]{:S(2)}) collective-permute-start(f32[8,12,120]{2,0,1:T(8,128)S(1)} %get-tuple-element.30), channel_id=1, source_target_pairs={{64,0},{128,64},{192,128},{256,192},{320,256},{384,320},{448,384},... | collective-permute-start | bytes 138248 | tf_op jit(solution)/shard_map/ppermute | solution.py:506
  60.0 1.4 copy-start
  61.9 6.3 %collective-permute-start.4 = (f32[3,12,48]{2,1,0:T(8,128)S(1)}, f32[3,12,48]{2,1,0:T(8,128)S(1)}, u32[]{:S(2)}, u32[]{:S(2)}) collective-permute-start(f32[3,12,48]{2,1,0:T(8,128)S(1)} %reshape.88), channel_id=1, source_target_pairs={{0,4},{4,8},{8,12},{12,16},{16,20},{20,24},{24,28},{28,32},{32,36}... | collective-permute-start | bytes 20744 | tf_op jit(solution)/shard_map/ppermute | solution.py:505
  63.9 12.4 %collective-permute-start.5 = (f32[3,12,48]{2,1,0:T(8,128)S(1)}, f32[3,12,48]{2,1,0:T(8,128)S(1)}, u32[]{:S(2)}, u32[]{:S(2)}) collective-permute-start(f32[3,12,48]{2,1,0:T(8,128)S(1)} %reshape.90), channel_id=1, source_target_pairs={{4,0},{8,4},{12,8},{16,12},{20,16},{24,20},{28,24},{32,28},{36,32}... | collective-permute-start | bytes 20744 | tf_op jit(solution)/shard_map/ppermute | solution.py:506
  76.8 4.5 %collective-permute-start.6 = (f32[3,12,120]{2,1,0:T(8,128)S(1)}, f32[3,12,120]{2,1,0:T(8,128)S(1)}, u32[]{:S(2)}, u32[]{:S(2)}) collective-permute-start(f32[3,12,120]{2,1,0:T(8,128)S(1)} %get-tuple-element.31), channel_id=1, source_target_pairs={{0,64},{64,128},{128,192},{192,256},{256,320},{320,384},{384,448},... | collective-permute-start | bytes 51848 | tf_op jit(solution)/shard_map/ppermute | solution.py:505
  76.8 4.4 %collective-permute-start.7 = (f32[3,12,120]{2,1,0:T(8,128)S(1)}, f32[3,12,120]{2,1,0:T(8,128)S(1)}, u32[]{:S(2)}, u32[]{:S(2)}) collective-permute-start(f32[3,12,120]{2,1,0:T(8,128)S(1)} %get-tuple-element.32), channel_id=1, source_target_pairs={{64,0},{128,64},{192,128},{256,192},{320,256},{384,320},{448,384},... | collective-permute-start | bytes 51848 | tf_op jit(solution)/shard_map/ppermute | solution.py:506
  81.4 1.6 %copy-start.1 = (f32[89,6,8,128]{3,2,1,0:T(8,128)S(1)}, f32[89,6,8,128]{3,2,1,0:T(8,128)}, u32[]{:S(2)}) copy-start(f32[89,6,8,128]{3,2,1,0:T(8,128)} %copy-done) | copy-start | bytes 6561796

commit v3 on v2

--- a/solution.py
+++ b/solution.py
@@ -157,20 +157,20 @@
                 own_sum[c, level] = acc[c]
             return carry
 
-        lax.fori_loop(0, HALF, per_level, 0, unroll=2)
+        lax.fori_loop(0, HALF, per_level, 0, unroll=6)
         spread(partner, depths, shift, partner_sum)
 
 
-def pack_kernel(spot_ref, polar_ref, direct_ref, group_ref, out_ref, rows):
+def pack_kernel(input_ref, out_ref, rows):
     site = lax.broadcasted_iota(jnp.int32, (1, ATOMS), 1)
     x = site // (LY * DEPTH)
     y = site // DEPTH - LY * x
     z = site - DEPTH * (site // DEPTH)
     for c, lattice in enumerate((x, y, z)):
-        rows[c : c + 1] = spot_ref[c, 0, 0] - lattice.astype(jnp.float32)
-        rows[4 + c : 5 + c] = polar_ref[0, 0] * direct_ref[c, 0, 0]
-    rows[3:4] = polar_ref[0, 0]
-    rows[7:8] = group_ref[0, 0].astype(jnp.float32)
+        rows[c : c + 1] = input_ref[c, 0, 0] - lattice.astype(jnp.float32)
+        rows[4 + c : 5 + c] = input_ref[3, 0, 0] * input_ref[4 + c, 0, 0]
+    rows[3:4] = input_ref[3, 0, 0]
+    rows[7:8] = input_ref[7, 0, 0]
     old = lax.broadcasted_iota(jnp.int32, (ATOMS, ATOMS), 0)
     new = lax.broadcasted_iota(jnp.int32, (ATOMS, ATOMS), 1)
     plane = new // (LX * LY)
@@ -240,7 +240,7 @@
                 own_sum[c, level] = acc[c]
             return carry
 
-        lax.fori_loop(0, HALF, per_level, 0, unroll=2)
+        lax.fori_loop(0, HALF, per_level, 0, unroll=6)
         spread(partner, depths, shift, partner_sum)
     finish(polar_of, own_sum, partner_sum, vec_b)
     moments = [inner(vec, vec, inverse_of), inner(vec, vec_b, inverse_of), inner(vec_b, vec_b, inverse_of)]
@@ -311,7 +311,9 @@
     moment_ref[...] = jnp.where(lane == 5, inner(vec, vec_b, inverse_of), moment_in[...])
 
 
-def gradient_kernel(moment_ref, far_ref, dipole_ref, force_ref, energy_ref, turned, out_ref):
+def gradient_kernel(
+    moment_ref, far_ref, dipole_ref, force_ref, energy_ref, turned, out_ref, wide
+):
     total = jnp.sum(moment_ref[...], axis=0, keepdims=True)
     lane = lax.broadcasted_iota(jnp.int32, (1, 128), 1)
 
@@ -331,19 +333,20 @@
     far_k1 = jnp.broadcast_to(k1, (1, 128))
     far_k2 = jnp.broadcast_to(k2, (1, 128))
 
+    for x in range(SPAN_X):
+        block = far_ref[x]
+        u = [[block[5 + 3 * q + c : 6 + 3 * q + c] for c in range(3)] for q in range(4)]
+        values = [block[c : c + 1] for c in range(5)]
+        values += [u[0][c] + far_k1 * u[1][c] + far_k2 * u[2][c] for c in range(3)]
+        values += [u[0][c] + u[1][c] + far_k1 * u[2][c] + far_k2 * u[3][c] for c in range(3)]
+        for n, value in enumerate(values):
+            wide[x, n] = jnp.broadcast_to(value, (8, 128))
+
     def plane(x, carry):
-        far = []
-        for n in range(2 * CUTOFF + 1):
-            block = far_ref[x + n]
-            spot = [block[c : c + 1] for c in range(5)]
-            u = [[block[5 + 3 * q + c : 6 + 3 * q + c] for c in range(3)] for q in range(4)]
-            dip = [u[0][c] + far_k1 * u[1][c] + far_k2 * u[2][c] for c in range(3)]
-            adj = [u[0][c] + u[1][c] + far_k1 * u[2][c] + far_k2 * u[3][c] for c in range(3)]
-            far.append((spot, dip, adj))
-        turned[...] = jnp.transpose(far_ref[x + CUTOFF])
+        turned[x] = jnp.transpose(far_ref[x + CUTOFF])
         for t in range(DEPTH):
             start = pl.multiple_of(x * (LY * DEPTH) + 8 * t, 8)
-            own_block = turned[pl.ds((t + CUTOFF) * SPAN_Y + CUTOFF, LY), :]
+            own_block = turned[x, pl.ds((t + CUTOFF) * SPAN_Y + CUTOFF, LY), :]
 
             def own_field(n):
                 return jnp.broadcast_to(own_block[:, n : n + 1], (8, 128))
@@ -354,7 +357,9 @@
             adj_i = [u[0][c] + u[1][c] + k1 * u[2][c] + k2 * u[3][c] for c in range(3)]
             acc = [jnp.zeros((8, 128), jnp.float32) for _ in range(3)]
             for n in range(2 * CUTOFF + 1):
-                spot, dip, adj = far[n]
+                spot = [wide[x + n, c] for c in range(5 if n == CUTOFF else 4)]
+                dip = [wide[x + n, 5 + c] for c in range(3)]
+                adj = [wide[x + n, 8 + c] for c in range(3)]
                 d = [spot[c] - spot_i[c] for c in range(3)]
                 s = d[0] * d[0] + d[1] * d[1] + d[2] * d[2]
                 if n == CUTOFF:
@@ -363,8 +368,8 @@
                 inv = lax.rsqrt(s)
                 inv2 = inv * inv
                 x_damp = (s * s * inv) * (spot_i[3] * spot[3])
-                xe = x_damp * jnp.exp(-x_damp)
                 e = jnp.exp(-x_damp)
+                xe = x_damp * e
                 l3 = 1.0 - e
                 l5 = l3 - xe
                 cut = jnp.maximum(1.0 - s * (1.0 / (CUTOFF * CUTOFF)), 0.0)
@@ -403,7 +408,7 @@
             out_ref[pl.ds(start, 8), :] = result
         return carry
 
-    lax.fori_loop(0, LX, plane, 0)
+    lax.fori_loop(0, LX, plane, 0, unroll=2)
     old = lax.broadcasted_iota(jnp.int32, (ATOMS, ATOMS), 0)
     new = lax.broadcasted_iota(jnp.int32, (ATOMS, ATOMS), 1)
     x = new // (LY * DEPTH)
@@ -445,11 +450,11 @@
     return pl.pallas_call(
         pack_kernel,
         out_shape=jax.ShapeDtypeStruct((LAYERS, 8, ATOMS), F32),
-        in_specs=vmem_specs(4),
+        in_specs=vmem_specs(1),
         out_specs=vmem_specs(1)[0],
         scratch_shapes=[pltpu.VMEM((8, ATOMS), F32)],
         compiler_params=PARAMS,
-    )(positions, polarizability, direct_field, groups)
+    )(jnp.concatenate([positions, polarizability[None], direct_field, groups[None].astype(F32)]))
 
 
 def run_first(base):
@@ -495,7 +500,11 @@
         ),
         in_specs=vmem_specs(2),
         out_specs=tuple(vmem_specs(3)),
-        scratch_shapes=[pltpu.VMEM((128, ROWS), F32), pltpu.VMEM((ATOMS, 128), F32)],
+        scratch_shapes=[
+            pltpu.VMEM((LX, 128, ROWS), F32),
+            pltpu.VMEM((ATOMS, 128), F32),
+            pltpu.VMEM((SPAN_X, 11, 8, 128), F32),
+        ],
         compiler_params=PARAMS,
     )(moments, far)
 

time: 140 us -> 131 us (0.936)
  Pallas kernels: 26.7 us -> 19.2 us
  local copies, waits for them, and re-layouts: 7.9 us -> 5.18 us
  other arithmetic: 0.66 us -> 2.07 us
    pallas_call x1, Pallas kernels: 14.3 us -> 9.71 us  [run_first(): pl.pallas_call(first_kernel, out_shape=outs, in_specs=vmem_specs(1), out_...]
    unnamed x14 -> x6, local copies, waits for them, and re-layouts: 5.69 us -> 2.98 us
    pallas_call x1, Pallas kernels: 6.71 us -> 4.21 us  [run_second(): pl.pallas_call(second_kernel, out_shape=outs, in_specs=[pl.BlockSpec(memo...]
where the time goes in v3:
time: 131 us; the launch traced here: 130 us
  blocking collectives  54.2 us (41%)
  starting transfers between devices  24.7 us (19%)
  waiting for transfers between devices  21.9 us (17%)
  Pallas kernels  19.2 us (15%)
  local copies, waits for them, and re-layouts  5.18 us (4%)
  between operations  2.72 us (2%)
  other arithmetic  2.07 us (2%)
    all_to_all x2, blocking collectives, on_device(): moments = lax.all_to_all(copies, axis, 0, 0).reshape(count, 128)  41.5 us
    ppermute x4, waiting for transfers between devices, both_sides(): lax.ppermute(low, axis, [((i + 1) % count, i) for i in range(count)])  18.6 us
    ppermute x4, starting transfers between devices, both_sides(): lax.ppermute(high, axis, [(i, (i + 1) % count) for i in range(count)])  13 us
    all_to_all x1, blocking collectives, on_device(): column = lax.all_to_all(copies, 'gz', 0, 0)  12.7 us
    ppermute x4, starting transfers between devices, both_sides(): lax.ppermute(low, axis, [((i + 1) % count, i) for i in range(count)])  11.7 us
    pallas_call x1, Pallas kernels, run_first(): pl.pallas_call(first_kernel, out_shape=outs, in_specs=vmem_specs(1), out_...  9.71 us
    pallas_call x1, Pallas kernels, run_gradient(): pl.pallas_call(gradient_kernel, out_shape=(jax.ShapeDtypeStruct((3, 1, 1,...  5.1 us
    pallas_call x1, Pallas kernels, run_second(): pl.pallas_call(second_kernel, out_shape=outs, in_specs=[pl.BlockSpec(memo...  4.21 us
  transfers between devices with their start and end apart: 8, of which 4 were waited for; matrix products, arithmetic and copies ran while one was open for 1% of the time, Pallas kernels for 0%

profile of v3, /device:TPU:6, one launch (start us, length us, event | category | flops | bytes accessed | tf_op | source)
XLA Modules:
  0.0 129.9 jit_solution(16778077141037201839)
XLA Ops:
  0.6 0.7 convert_bitcast_fusion
  1.3 0.7 pad_maximum_fusion.2.input_ref
  2.0 0.2 shard_map.76
  2.3 12.7 %all_to_all.15 = f32[4,8,192]{2,1,0:T(8,128)S(1)} all-to-all(f32[4,8,192]{2,1,0:T(8,128)S(1)} %shard_map.76), channel_id=1, replica_groups=mesh['gx'=16,'gy'=16,'gz'=4] {'gz'}, dimensions={0} | all-to-all | bytes 49152 | tf_op jit(solution)/shard_map/all_to_all | solution.py:552
  15.0 10.8 %collective-permute-start = (f32[4,8,192]{2,1,0:T(8,128)S(1)}, f32[4,8,192]{2,1,0:T(8,128)S(1)}, u32[]{:S(2)}, u32[]{:S(2)}) collective-permute-start(f32[4,8,192]{2,1,0:T(8,128)S(1)} %all_to_all.15), channel_id=1, source_target_pairs={{0,4},{4,8},{8,12},{12,16},{16,20},{20,24},{24,28},{28,32},{32,36}... | collective-permute-start | bytes 73736 | tf_op jit(solution)/shard_map/ppermute | solution.py:514
  25.8 1.9 %collective-permute-start.1 = (f32[4,8,192]{2,1,0:T(8,128)S(1)}, f32[4,8,192]{2,1,0:T(8,128)S(1)}, u32[]{:S(2)}, u32[]{:S(2)}) collective-permute-start(f32[4,8,192]{2,1,0:T(8,128)S(1)} %all_to_all.15), channel_id=1, source_target_pairs={{4,0},{8,4},{12,8},{16,12},{20,16},{24,20},{28,24},{32,28},{36,32}... | collective-permute-start | bytes 73736 | tf_op jit(solution)/shard_map/ppermute | solution.py:515
  27.7 0.2 reshape.91
  27.9 0.2 reshape.89
  28.3 10.3 %collective-permute-done.1 = f32[4,8,192]{2,1,0:T(8,128)S(1)} collective-permute-done((f32[4,8,192]{2,1,0:T(8,128)S(1)}, f32[4,8,192]{2,1,0:T(8,128)S(1)}, u32[]{:S(2)}, u32[]{:S(2)}) %collective-permute-start.1) | collective-permute-done | bytes 24608 | tf_op jit(solution)/shard_map/ppermute | solution.py:515
  38.9 0.3 pad_maximum_fusion
  39.5 3.0 %collective-permute-start.3 = (f32[8,12,120]{2,0,1:T(8,128)S(1)}, f32[8,12,120]{2,0,1:T(8,128)S(1)}, u32[]{:S(2)}, u32[]{:S(2)}) collective-permute-start(f32[8,12,120]{2,0,1:T(8,128)S(1)} %get-tuple-element.30), channel_id=1, source_target_pairs={{64,0},{128,64},{192,128},{256,192},{320,256},{384,320},{448,384},... | collective-permute-start | bytes 138248 | tf_op jit(solution)/shard_map/ppermute | solution.py:515
  42.4 1.8 %collective-permute-done.2 = f32[8,12,120]{2,0,1:T(8,128)S(1)} collective-permute-done((f32[8,12,120]{2,0,1:T(8,128)S(1)}, f32[8,12,120]{2,0,1:T(8,128)S(1)}, u32[]{:S(2)}, u32[]{:S(2)}) %collective-permute-start.2) | collective-permute-done | bytes 46112 | tf_op jit(solution)/shard_map/ppermute | solution.py:514
  44.4 9.7 %shard_map.77 = (f32[89,6,8,128]{3,2,1,0:T(8,128)S(1)}, f32[89,6,8,128]{3,2,1,0:T(8,128)S(1)}, f32[3,6,8,128]{3,2,1,0:T(8,128)S(1)}, f32[3,6,8,128]{3,2,1,0:T(8,128)S(1)}, f32[1,128]{1,0:T(1,128)S(1)}) custom-call(f32[8,6,8,128]{3,2,1,0:T(8,128)S(1)} %bitcast.37), custom_call_target="tpu_custom_call" | custom-call | tf_op jit(solution)/shard_map/pallas_call | solution.py:468
  54.1 1.4 %copy-done = f32[89,6,8,128]{3,2,1,0:T(8,128)} copy-done((f32[89,6,8,128]{3,2,1,0:T(8,128)}, f32[89,6,8,128]{3,2,1,0:T(8,128)S(1)}, u32[]{:S(2)}) %copy-start) | copy-done | bytes 2187288
  56.0 2.1 %collective-permute-start.4 = (f32[3,12,48]{2,1,0:T(8,128)S(1)}, f32[3,12,48]{2,1,0:T(8,128)S(1)}, u32[]{:S(2)}, u32[]{:S(2)}) collective-permute-start(f32[3,12,48]{2,1,0:T(8,128)S(1)} %reshape.101), channel_id=1, source_target_pairs={{0,4},{4,8},{8,12},{12,16},{16,20},{20,24},{24,28},{28,32},{32,36}... | collective-permute-start | bytes 20744 | tf_op jit(solution)/shard_map/ppermute | solution.py:514
  58.3 3.9 %collective-permute-start.5 = (f32[3,12,48]{2,1,0:T(8,128)S(1)}, f32[3,12,48]{2,1,0:T(8,128)S(1)}, u32[]{:S(2)}, u32[]{:S(2)}) collective-permute-start(f32[3,12,48]{2,1,0:T(8,128)S(1)} %reshape.103), channel_id=1, source_target_pairs={{4,0},{8,4},{12,8},{16,12},{20,16},{24,20},{28,24},{32,28},{36,32}... | collective-permute-start | bytes 20744 | tf_op jit(solution)/shard_map/ppermute | solution.py:515
  62.4 8.2 %collective-permute-done.5 = f32[3,12,48]{2,1,0:T(8,128)S(1)} collective-permute-done((f32[3,12,48]{2,1,0:T(8,128)S(1)}, f32[3,12,48]{2,1,0:T(8,128)S(1)}, u32[]{:S(2)}, u32[]{:S(2)}) %collective-permute-start.5) | collective-permute-done | bytes 6944 | tf_op jit(solution)/shard_map/ppermute | solution.py:515
  71.1 2.9 %collective-permute-start.7 = (f32[3,12,120]{2,1,0:T(8,128)S(1)}, f32[3,12,120]{2,1,0:T(8,128)S(1)}, u32[]{:S(2)}, u32[]{:S(2)}) collective-permute-start(f32[3,12,120]{2,1,0:T(8,128)S(1)} %get-tuple-element.32), channel_id=1, source_target_pairs={{64,0},{128,64},{192,128},{256,192},{320,256},{384,320},{448,384},... | collective-permute-start | bytes 51848 | tf_op jit(solution)/shard_map/ppermute | solution.py:515
  74.0 1.5 %collective-permute-done.6 = f32[3,12,120]{2,1,0:T(8,128)S(1)} collective-permute-done((f32[3,12,120]{2,1,0:T(8,128)S(1)}, f32[3,12,120]{2,1,0:T(8,128)S(1)}, u32[]{:S(2)}, u32[]{:S(2)}) %collective-permute-start.6) | collective-permute-done | bytes 17312 | tf_op jit(solution)/shard_map/ppermute | solution.py:514
  75.7 1.6 %copy-done.1 = f32[89,6,8,128]{3,2,1,0:T(8,128)S(1)} copy-done((f32[89,6,8,128]{3,2,1,0:T(8,128)S(1)}, f32[89,6,8,128]{3,2,1,0:T(8,128)}, u32[]{:S(2)}) %copy-start.1) | copy-done | bytes 2187288
  77.3 4.2 %shard_map.78 = (f32[14,24,128]{2,1,0:T(8,128)S(1)}, f32[1,128]{1,0:T(1,128)S(1)}) custom-call(s32[1]{0:T(128)} %bitcast.layer_ref, f32[8,6,8,128]{3,2,1,0:T(8,128)S(1)} %bitcast.38, f32[89,6,8,128]{3,2,1,0:T(8,128)S(1)} %get-tuple-element.15.c3_ref, f32[89,6,8,128]{3,2,1,0:T(8,128)S(1)} %copy-done.1, f32[3,6,8,128]{3,2,1,0:T(8,128)S(1)} %get-tuple-element.17.u1_ref, ...), custom_call_target="tpu_custom_call" | custom-call | tf_op jit(solution)/shard_map/pallas_call | solution.py:483
  81.6 14.3 %all_to_all.16 = f32[16,1,128]{2,1,0:T(1,128)S(1)} all-to-all(f32[16,1,128]{2,1,0:T(1,128)S(1)} %broadcast_in_dim.23), channel_id=1, replica_groups=mesh['gx'=16,'gy'=16,'gz'=4] {'gx'}, dimensions={0} | all-to-all | bytes 16384 | tf_op jit(solution)/shard_map/all_to_all | solution.py:574
  95.9 27.1 %all_to_all.17 = f32[16,1,128]{2,1,0:T(1,128)S(1)} all-to-all(f32[16,1,128]{2,1,0:T(1,128)S(1)} %broadcast_in_dim.24), channel_id=1, replica_groups=mesh['gx'=16,'gy'=16,'gz'=4] {'gy'}, dimensions={0} | all-to-all | bytes 16384 | tf_op jit(solution)/shard_map/all_to_all | solution.py:574
  123.0 5.1 %shard_map.79 = (f32[3,1,1,1,192]{4,3,2,1,0:T(1,128)}, f32[3,1,1,1,192]{4,3,2,1,0:T(1,128)}, f32[1,1]{1,0:T(1,128)}) custom-call(f32[16,128]{1,0:T(8,128)S(1)} %bitcast.40, f32[14,24,128]{2,1,0:T(8,128)S(1)} %get-tuple-element.23.far_ref), custom_call_target="tpu_custom_call" | custom-call | tf_op jit(solution)/shard_map/pallas_call | solution.py:494
  (40 shorter events, 2.4 us)
Async XLA Ops:
  15.0 13.0 %collective-permute-start = (f32[4,8,192]{2,1,0:T(8,128)S(1)}, f32[4,8,192]{2,1,0:T(8,128)S(1)}, u32[]{:S(2)}, u32[]{:S(2)}) collective-permute-start(f32[4,8,192]{2,1,0:T(8,128)S(1)} %all_to_all.15), channel_id=1, source_target_pairs={{0,4},{4,8},{8,12},{12,16},{16,20},{20,24},{24,28},{28,32},{32,36}... | collective-permute-start | bytes 73736 | tf_op jit(solution)/shard_map/ppermute | solution.py:514
  25.8 12.9 %collective-permute-start.1 = (f32[4,8,192]{2,1,0:T(8,128)S(1)}, f32[4,8,192]{2,1,0:T(8,128)S(1)}, u32[]{:S(2)}, u32[]{:S(2)}) collective-permute-start(f32[4,8,192]{2,1,0:T(8,128)S(1)} %all_to_all.15), channel_id=1, source_target_pairs={{4,0},{8,4},{12,8},{16,12},{20,16},{24,20},{28,24},{32,28},{36,32}... | collective-permute-start | bytes 73736 | tf_op jit(solution)/shard_map/ppermute | solution.py:515
  28.2 16.1 %copy-start.2 = (f32[8,12,512]{2,0,1:T(8,128)S(1)}, f32[8,12,512]{2,0,1:T(8,128)}, u32[]{:S(2)}) copy-start(f32[8,12,512]{2,0,1:T(8,128)} %constant.24) | copy-start | bytes 589828
  39.5 4.7 %collective-permute-start.2 = (f32[8,12,120]{2,0,1:T(8,128)S(1)}, f32[8,12,120]{2,0,1:T(8,128)S(1)}, u32[]{:S(2)}, u32[]{:S(2)}) collective-permute-start(f32[8,12,120]{2,0,1:T(8,128)S(1)} %get-tuple-element.29), channel_id=1, source_target_pairs={{0,64},{64,128},{128,192},{192,256},{256,320},{320,384},{384,448},... | collective-permute-start | bytes 138248 | tf_op jit(solution)/shard_map/ppermute | solution.py:514
  39.5 4.7 %collective-permute-start.3 = (f32[8,12,120]{2,0,1:T(8,128)S(1)}, f32[8,12,120]{2,0,1:T(8,128)S(1)}, u32[]{:S(2)}, u32[]{:S(2)}) collective-permute-start(f32[8,12,120]{2,0,1:T(8,128)S(1)} %get-tuple-element.30), channel_id=1, source_target_pairs={{64,0},{128,64},{192,128},{256,192},{320,256},{384,320},{448,384},... | collective-permute-start | bytes 138248 | tf_op jit(solution)/shard_map/ppermute | solution.py:515
  54.1 1.4 %copy-start = (f32[89,6,8,128]{3,2,1,0:T(8,128)}, f32[89,6,8,128]{3,2,1,0:T(8,128)S(1)}, u32[]{:S(2)}) copy-start(f32[89,6,8,128]{3,2,1,0:T(8,128)S(1)} %get-tuple-element.16.c5_ref) | copy-start | bytes 6561796
  56.0 6.3 %collective-permute-start.4 = (f32[3,12,48]{2,1,0:T(8,128)S(1)}, f32[3,12,48]{2,1,0:T(8,128)S(1)}, u32[]{:S(2)}, u32[]{:S(2)}) collective-permute-start(f32[3,12,48]{2,1,0:T(8,128)S(1)} %reshape.101), channel_id=1, source_target_pairs={{0,4},{4,8},{8,12},{12,16},{16,20},{20,24},{24,28},{28,32},{32,36}... | collective-permute-start | bytes 20744 | tf_op jit(solution)/shard_map/ppermute | solution.py:514
  58.3 12.4 %collective-permute-start.5 = (f32[3,12,48]{2,1,0:T(8,128)S(1)}, f32[3,12,48]{2,1,0:T(8,128)S(1)}, u32[]{:S(2)}, u32[]{:S(2)}) collective-permute-start(f32[3,12,48]{2,1,0:T(8,128)S(1)} %reshape.103), channel_id=1, source_target_pairs={{4,0},{8,4},{12,8},{16,12},{20,16},{24,20},{28,24},{32,28},{36,32}... | collective-permute-start | bytes 20744 | tf_op jit(solution)/shard_map/ppermute | solution.py:515
  71.1 4.5 %collective-permute-start.6 = (f32[3,12,120]{2,1,0:T(8,128)S(1)}, f32[3,12,120]{2,1,0:T(8,128)S(1)}, u32[]{:S(2)}, u32[]{:S(2)}) collective-permute-start(f32[3,12,120]{2,1,0:T(8,128)S(1)} %get-tuple-element.31), channel_id=1, source_target_pairs={{0,64},{64,128},{128,192},{192,256},{256,320},{320,384},{384,448},... | collective-permute-start | bytes 51848 | tf_op jit(solution)/shard_map/ppermute | solution.py:514
  71.1 4.4 %collective-permute-start.7 = (f32[3,12,120]{2,1,0:T(8,128)S(1)}, f32[3,12,120]{2,1,0:T(8,128)S(1)}, u32[]{:S(2)}, u32[]{:S(2)}) collective-permute-start(f32[3,12,120]{2,1,0:T(8,128)S(1)} %get-tuple-element.32), channel_id=1, source_target_pairs={{64,0},{128,64},{192,128},{256,192},{320,256},{384,320},{448,384},... | collective-permute-start | bytes 51848 | tf_op jit(solution)/shard_map/ppermute | solution.py:515
  75.7 1.6 %copy-start.1 = (f32[89,6,8,128]{3,2,1,0:T(8,128)S(1)}, f32[89,6,8,128]{3,2,1,0:T(8,128)}, u32[]{:S(2)}) copy-start(f32[89,6,8,128]{3,2,1,0:T(8,128)} %copy-done) | copy-start | bytes 6561796
